TPU v7x, 32 devices: a whole 2x2x4 slice. The times are simulated.
32 devices in a mesh: groups: 2 (over y), wide: 4 (over z), narrow: 2 (over x), pair: 2 (over core).
Axes of the slice: x: 2, y: 2, z: 4, core: 2. Of those that a mesh axis runs over, the one named last changes fastest.
Arguments:
- volume: bfloat16 [48, 16, 64, 128], P(('groups', 'wide'), 'narrow', 'pair'), parts along dimension 0, may hold values from -6 to 6
- w_encode: bfloat16 [3, 3, 3, 128, 128], replicated, may hold values from -0.109375 to 0.109375
- b_encode: float32 [128], replicated, may hold values from -3 to 3
- w_down: bfloat16 [2, 2, 2, 128, 256], replicated, may hold values from -0.1875 to 0.1875
- b_down: float32 [256], replicated, may hold values from -3 to 3
- w_bottom: bfloat16 [3, 3, 3, 256, 256], replicated, may hold values from -0.078125 to 0.078125
- b_bottom: float32 [256], replicated, may hold values from -3 to 3
- w_up: bfloat16 [2, 2, 2, 256, 128], replicated, may hold values from -0.375 to 0.375
- b_up: float32 [128], replicated, may hold values from -3 to 3
- w_decode: bfloat16 [3, 3, 3, 256, 128], replicated, may hold values from -0.078125 to 0.078125
- b_decode: float32 [128], replicated, may hold values from -3 to 3
Outputs:
- decoded: bfloat16 [48, 16, 64, 128], P(('groups', 'wide'), 'narrow', 'pair'), parts along dimension 0
There are 2 independent parts, one for each index of `groups`. A program takes and returns all parts, laid end to end along the dimension named above; an argument that names none is the same for every part. Nothing has to cross between parts.
All inputs are finite; a program needn't handle non-finite values.
Results may differ from a plain program's by a relative error of at most 0.008.
Values may be sent and summed in bfloat16 or wider, within the bound.
A program may use at most 64 MiB of HBM per device.

v0:
```python
import jax
import jax.numpy as jnp
from jax import lax
from jax.sharding import PartitionSpec as P

leak_slope = 0.01


def padded_2(block, sides, width):
    for axis, dim in sides:
        count = lax.axis_size(axis)
        forward = [(i, i + 1) for i in range(count - 1)]
        backward = [(target, source) for source, target in forward]
        low = lax.ppermute(
            lax.slice_in_dim(block, block.shape[dim] - width, None, axis=dim), axis, forward
        )
        high = lax.ppermute(lax.slice_in_dim(block, 0, width, axis=dim), axis, backward)
        block = jnp.concatenate([low, block, high], axis=dim)
    return block


def leaky_relu(values):
    return jnp.maximum(values, leak_slope * values)


def conv_taps(padded, weight, first_cells, second_cells, third_cells):
    channels = padded.shape[-1]
    outputs = weight.shape[-1]
    summed = jnp.zeros((first_cells * second_cells * third_cells, outputs), jnp.float32)
    for offset_a in range(3):
        window_rows = jnp.concatenate(
            [
                padded[
                    offset_a : offset_a + first_cells,
                    offset_b : offset_b + second_cells,
                    offset_c : offset_c + third_cells,
                ]
                for offset_b in range(3)
                for offset_c in range(3)
            ],
            axis=-1,
        )
        summed = summed + jnp.dot(
            window_rows.reshape(-1, 9 * channels),
            weight[offset_a].reshape(9 * channels, outputs),
            preferred_element_type=jnp.float32,
        )
    return summed


def body(
    volume, w_encode, b_encode, w_down, b_down, w_bottom, b_bottom, w_up, b_up, w_decode, b_decode
):
    depth_cells, height_cells, width_cells, skip_width = volume.shape
    deep_width = w_down.shape[4]
    half_depth, half_height, half_width = (depth_cells // 2, height_cells // 2, width_cells // 2)
    framed_input = padded_2(volume, (("wide", 0), ("narrow", 1), ("pair", 2)), 1)
    encoded = leaky_relu(
        conv_taps(framed_input, w_encode, depth_cells, height_cells, width_cells) + b_encode
    )
    encoded = encoded.astype(jnp.bfloat16).reshape(
        depth_cells, height_cells, width_cells, skip_width
    )
    blocks = encoded.reshape(half_depth, 2, half_height, 2, half_width, 2, skip_width)
    blocks = blocks.transpose(0, 2, 4, 1, 3, 5, 6).reshape(
        half_depth * half_height * half_width, 8 * skip_width
    )
    coarse = jnp.dot(
        blocks, w_down.reshape(8 * skip_width, deep_width), preferred_element_type=jnp.float32
    )
    coarse = (
        leaky_relu(coarse + b_down)
        .astype(jnp.bfloat16)
        .reshape(half_depth, half_height, half_width, deep_width)
    )
    coarse_padded = padded_2(coarse, (("wide", 0), ("narrow", 1), ("pair", 2)), 1)
    summed = conv_taps(coarse_padded, w_bottom, half_depth, half_height, half_width)
    bottom = (
        leaky_relu(summed + b_bottom)
        .astype(jnp.bfloat16)
        .reshape(half_depth, half_height, half_width, deep_width)
    )
    up_matrix = jnp.transpose(w_up, (3, 0, 1, 2, 4)).reshape(deep_width, 8 * skip_width)
    lifted = jnp.dot(bottom.reshape(-1, deep_width), up_matrix, preferred_element_type=jnp.float32)
    lifted = lifted + jnp.tile(b_up, 8)
    raised = lifted.astype(jnp.bfloat16).reshape(
        half_depth, half_height, half_width, 2, 2, 2, skip_width
    )
    raised = raised.transpose(0, 3, 1, 4, 2, 5, 6).reshape(
        depth_cells, height_cells, width_cells, skip_width
    )
    joined = padded_2(
        jnp.concatenate([raised, encoded], axis=-1), (("wide", 0), ("narrow", 1), ("pair", 2)), 1
    )
    decoded = leaky_relu(
        conv_taps(joined, w_decode, depth_cells, height_cells, width_cells) + b_decode
    )
    return decoded.astype(jnp.bfloat16).reshape(depth_cells, height_cells, width_cells, skip_width)


def solution(mesh):
    return jax.shard_map(
        body,
        mesh=mesh,
        in_specs=(
            P(("groups", "wide"), "narrow", "pair", None),
            P(),
            P(),
            P(),
            P(),
            P(),
            P(),
            P(),
            P(),
            P(),
            P(),
        ),
        out_specs=P(("groups", "wide"), "narrow", "pair", None),
        check_vma=False,
    )
```

profile of v0, /device:TPU:0, one launch (start us, length us, event | category | flops | bytes accessed | tf_op | source)
XLA Modules:
  0.0 97.7 jit_solution(7281089214132819046)
XLA Ops:
  0.9 4.9 %collective-permute-start = (bf16[1,8,32,128]{3,2,1,0:T(8,128)(2,1)S(1)}, bf16[1,8,32,128]{3,2,1,0:T(8,128)(2,1)S(1)}, u32[]{:S(2)}, u32[]{:S(2)}) collective-permute-start(bf16[1,8,32,128]{3,2,1,0:T(8,128)(2,1)S(1)} %get-tuple-element.84), channel_id=1, source_target_pairs={{0,4},{4,8},{8,12},{1,5},{5,9},{9,13},{2,6},{6,10},{10,14},{3,7},{... | collective-permute-start | bytes 196616 | tf_op jit(solution)/shard_map/ppermute | solution.py:14
  5.9 1.3 %collective-permute-start.1 = (bf16[1,8,32,128]{3,2,1,0:T(8,128)(2,1)S(1)}, bf16[1,8,32,128]{3,2,1,0:T(8,128)(2,1)S(1)}, u32[]{:S(2)}, u32[]{:S(2)}) collective-permute-start(bf16[1,8,32,128]{3,2,1,0:T(8,128)(2,1)S(1)} %get-tuple-element.83), channel_id=1, source_target_pairs={{4,0},{8,4},{12,8},{5,1},{9,5},{13,9},{6,2},{10,6},{14,10},{7,3},{... | collective-permute-start | bytes 196616 | tf_op jit(solution)/shard_map/ppermute | solution.py:17
  8.8 3.2 %collective-permute-done.1 = bf16[1,8,32,128]{3,2,1,0:T(8,128)(2,1)S(1)} collective-permute-done((bf16[1,8,32,128]{3,2,1,0:T(8,128)(2,1)S(1)}, bf16[1,8,32,128]{3,2,1,0:T(8,128)(2,1)S(1)}, u32[]{:S(2)}, u32[]{:S(2)}) %collective-permute-start.1) | collective-permute-done | bytes 65568 | tf_op jit(solution)/shard_map/ppermute | solution.py:17
  12.1 1.3 %collective-permute-start.3 = (bf16[8,1,32,128]{3,2,1,0:T(8,128)(2,1)S(1)}, bf16[8,1,32,128]{3,2,1,0:T(8,128)(2,1)S(1)}, u32[]{:S(2)}, u32[]{:S(2)}) collective-permute-start(bf16[8,1,32,128]{3,2,1,0:T(8,128)(2,1)S(1)} %get-tuple-element.79), channel_id=1, source_target_pairs={{2,0},{3,1},{6,4},{7,5},{10,8},{11,9},{14,12},{15,13},{18,16},{19,... | collective-permute-start | bytes 196616 | tf_op jit(solution)/shard_map/ppermute | solution.py:17
  13.4 4.5 %collective-permute-start.2 = (bf16[8,1,32,128]{3,2,1,0:T(8,128)(2,1)S(1)}, bf16[8,1,32,128]{3,2,1,0:T(8,128)(2,1)S(1)}, u32[]{:S(2)}, u32[]{:S(2)}) collective-permute-start(bf16[8,1,32,128]{3,2,1,0:T(8,128)(2,1)S(1)} %get-tuple-element.78), channel_id=1, source_target_pairs={{0,2},{1,3},{4,6},{5,7},{8,10},{9,11},{12,14},{13,15},{16,18},{17,... | collective-permute-start | bytes 196616 | tf_op jit(solution)/shard_map/ppermute | solution.py:14
  18.2 1.6 %collective-permute-done.2 = bf16[8,1,32,128]{3,2,1,0:T(8,128)(2,1)S(1)} collective-permute-done((bf16[8,1,32,128]{3,2,1,0:T(8,128)(2,1)S(1)}, bf16[8,1,32,128]{3,2,1,0:T(8,128)(2,1)S(1)}, u32[]{:S(2)}, u32[]{:S(2)}) %collective-permute-start.2) | collective-permute-done | bytes 65568 | tf_op jit(solution)/shard_map/ppermute | solution.py:14
  19.9 1.3 %collective-permute-start.5 = (bf16[8,10,1,128]{3,2,1,0:T(2,128)(2,1)S(1)}, bf16[8,10,1,128]{3,2,1,0:T(2,128)(2,1)S(1)}, u32[]{:S(2)}, u32[]{:S(2)}) collective-permute-start(bf16[8,10,1,128]{3,2,1,0:T(2,128)(2,1)S(1)} %get-tuple-element.70), channel_id=1, source_target_pairs={{1,0},{3,2},{5,4},{7,6},{9,8},{11,10},{13,12},{15,14},{17,16},{19,... | collective-permute-start | bytes 61448 | tf_op jit(solution)/shard_map/ppermute | solution.py:17
  21.2 3.0 %collective-permute-start.4 = (bf16[8,10,1,128]{3,2,1,0:T(2,128)(2,1)S(1)}, bf16[8,10,1,128]{3,2,1,0:T(2,128)(2,1)S(1)}, u32[]{:S(2)}, u32[]{:S(2)}) collective-permute-start(bf16[8,10,1,128]{3,2,1,0:T(2,128)(2,1)S(1)} %get-tuple-element.71), channel_id=1, source_target_pairs={{0,1},{2,3},{4,5},{6,7},{8,9},{10,11},{12,13},{14,15},{16,17},{18,... | collective-permute-start | bytes 61448 | tf_op jit(solution)/shard_map/ppermute | solution.py:14
  24.2 1.2 %fusion.27 = (bf16[1,3,3,128,128]{4,3,2,1,0:T(8,128)(2,1)S(1)}, bf16[1,3,3,128,128]{4,3,2,1,0:T(8,128)(2,1)S(1)}, bf16[1,3,3,128,128]{4,3,2,1,0:T(8,128)(2,1)S(1)}) fusion(bf16[3,3,3,128,128]{4,3,2,1,0:T(8,128)(2,1)} %param.12), kind=kLoop, calls=%fused_computation.167 | loop fusion | bytes 1769472 | tf_op jit(solution)/shard_map/slice | solution.py:45
  30.9 1.1 %convolution_add_fusion.1 = f32[1536,128]{1,0:T(8,128)S(1)} fusion(f32[1536,128]{1,0:T(8,128)S(1)} %fusion.31, bf16[1536,1152]{1,0:T(8,128)(2,1)S(1)} %bitcast.88, bf16[1152,128]{1,0:T(8,128)(2,1)S(1)} %bitcast.109), kind=kOutput, calls=%fused_computation.2 | convolution fusion | flops 453181440 | bytes 5406720 | tf_op jit(solution)/shard_map/dot_general | solution.py:43
  34.1 1.3 %collective-permute-start.7 = (bf16[1,4,16,256]{3,2,1,0:T(8,128)(2,1)S(1)}, bf16[1,4,16,256]{3,2,1,0:T(8,128)(2,1)S(1)}, u32[]{:S(2)}, u32[]{:S(2)}) collective-permute-start(bf16[1,4,16,256]{3,2,1,0:T(8,128)(2,1)S(1)} %bitcast.128), channel_id=1, source_target_pairs={{4,0},{8,4},{12,8},{5,1},{9,5},{13,9},{6,2},{10,6},{14,10},{7,3},{... | collective-permute-start | bytes 98312 | tf_op jit(solution)/shard_map/ppermute | solution.py:17
  35.4 4.5 %collective-permute-start.6 = (bf16[1,4,16,256]{3,2,1,0:T(8,128)(2,1)S(1)}, bf16[1,4,16,256]{3,2,1,0:T(8,128)(2,1)S(1)}, u32[]{:S(2)}, u32[]{:S(2)}) collective-permute-start(bf16[1,4,16,256]{3,2,1,0:T(8,128)(2,1)S(1)} %bitcast.127), channel_id=1, source_target_pairs={{0,4},{4,8},{8,12},{1,5},{5,9},{9,13},{2,6},{6,10},{10,14},{3,7},{... | collective-permute-start | bytes 98312 | tf_op jit(solution)/shard_map/ppermute | solution.py:14
  40.0 3.4 %fusion.25 = (bf16[1,3,3,256,256]{4,3,2,1,0:T(8,128)(2,1)}, bf16[1,3,3,256,256]{4,3,2,1,0:T(8,128)(2,1)S(1)}, bf16[1,3,3,256,256]{4,3,2,1,0:T(8,128)(2,1)S(1)}) fusion(bf16[3,3,3,256,256]{4,3,2,1,0:T(8,128)(2,1)} %param.16), kind=kLoop, calls=%fused_computation.165 | loop fusion | bytes 7077888 | tf_op jit(solution)/shard_map/slice | solution.py:45
  43.4 1.3 %collective-permute-start.9 = (bf16[5,1,16,256]{3,2,1,0:T(8,128)(2,1)S(1)}, bf16[5,1,16,256]{3,2,1,0:T(8,128)(2,1)S(1)}, u32[]{:S(2)}, u32[]{:S(2)}) collective-permute-start(bf16[5,1,16,256]{3,2,1,0:T(8,128)(2,1)S(1)} %get-tuple-element.116), channel_id=1, source_target_pairs={{2,0},{3,1},{6,4},{7,5},{10,8},{11,9},{14,12},{15,13},{18,16},{19,... | collective-permute-start | bytes 122888 | tf_op jit(solution)/shard_map/ppermute | solution.py:17
  44.7 4.5 %collective-permute-start.8 = (bf16[5,1,16,256]{3,2,1,0:T(8,128)(2,1)S(1)}, bf16[5,1,16,256]{3,2,1,0:T(8,128)(2,1)S(1)}, u32[]{:S(2)}, u32[]{:S(2)}) collective-permute-start(bf16[5,1,16,256]{3,2,1,0:T(8,128)(2,1)S(1)} %get-tuple-element.115), channel_id=1, source_target_pairs={{0,2},{1,3},{4,6},{5,7},{8,10},{9,11},{12,14},{13,15},{16,18},{17,... | collective-permute-start | bytes 122888 | tf_op jit(solution)/shard_map/ppermute | solution.py:14
  49.2 2.0 %copy.14 = bf16[2,2,2,256,128]{3,4,2,1,0:T(8,128)(2,1)} copy(bf16[2,2,2,256,128]{4,3,2,1,0:T(8,128)(2,1)} %param.18) | data formatting | bytes 1048576 | tf_op args[7]
  51.3 1.3 %collective-permute-start.11 = (bf16[5,6,1,256]{3,2,1,0:T(2,128)(2,1)S(1)}, bf16[5,6,1,256]{3,2,1,0:T(2,128)(2,1)S(1)}, u32[]{:S(2)}, u32[]{:S(2)}) collective-permute-start(bf16[5,6,1,256]{3,2,1,0:T(2,128)(2,1)S(1)} %get-tuple-element.105), channel_id=1, source_target_pairs={{1,0},{3,2},{5,4},{7,6},{9,8},{11,10},{13,12},{15,14},{17,16},{19,... | collective-permute-start | bytes 46088 | tf_op jit(solution)/shard_map/ppermute | solution.py:17
  52.6 3.0 %collective-permute-start.10 = (bf16[5,6,1,256]{3,2,1,0:T(2,128)(2,1)S(1)}, bf16[5,6,1,256]{3,2,1,0:T(2,128)(2,1)S(1)}, u32[]{:S(2)}, u32[]{:S(2)}) collective-permute-start(bf16[5,6,1,256]{3,2,1,0:T(2,128)(2,1)S(1)} %get-tuple-element.106), channel_id=1, source_target_pairs={{0,1},{2,3},{4,5},{6,7},{8,9},{10,11},{12,13},{14,15},{16,17},{18,... | collective-permute-start | bytes 46088 | tf_op jit(solution)/shard_map/ppermute | solution.py:14
  58.5 2.4 %fusion.2 = bf16[192,1024]{1,0:T(8,128)(2,1)S(1)} fusion(bf16[256,1024]{0,1:T(8,128)(2,1)S(1)} %bitcast.107, f32[1024]{0:T(1024)S(1)} %broadcast_bitcast_fusion, f32[192,256]{1,0:T(8,128)S(1)} %convolution_add_fusion.7, bf16[192,2304]{1,0:T(8,128)(2,1)} %bitcast.111, bf16[2304,256]{1,0:T(8,128)(2,1)} %bitcast.97, f32[256]{0:T(256)S(1)} %copy-done.6), kind=kOutput, calls=%fused_computation.9 | convolution fusion | flops 327794688 | bytes 3183616 | tf_op jit(solution)/shard_map/dot_general | solution.py:84
  61.6 1.3 %collective-permute-start.13 = (bf16[1,8,32,256]{3,2,1,0:T(8,128)(2,1)S(1)}, bf16[1,8,32,256]{3,2,1,0:T(8,128)(2,1)S(1)}, u32[]{:S(2)}, u32[]{:S(2)}) collective-permute-start(bf16[1,8,32,256]{3,2,1,0:T(8,128)(2,1)S(1)} %get-tuple-element.67), channel_id=1, source_target_pairs={{4,0},{8,4},{12,8},{5,1},{9,5},{13,9},{6,2},{10,6},{14,10},{7,3},{... | collective-permute-start | bytes 393224 | tf_op jit(solution)/shard_map/ppermute | solution.py:17
  62.9 4.6 %collective-permute-start.12 = (bf16[1,8,32,256]{3,2,1,0:T(8,128)(2,1)S(1)}, bf16[1,8,32,256]{3,2,1,0:T(8,128)(2,1)S(1)}, u32[]{:S(2)}, u32[]{:S(2)}) collective-permute-start(bf16[1,8,32,256]{3,2,1,0:T(8,128)(2,1)S(1)} %get-tuple-element.66), channel_id=1, source_target_pairs={{0,4},{4,8},{8,12},{1,5},{5,9},{9,13},{2,6},{6,10},{10,14},{3,7},{... | collective-permute-start | bytes 393224 | tf_op jit(solution)/shard_map/ppermute | solution.py:14
  67.5 1.8 %collective-permute-done.13 = bf16[1,8,32,256]{3,2,1,0:T(8,128)(2,1)S(1)} collective-permute-done((bf16[1,8,32,256]{3,2,1,0:T(8,128)(2,1)S(1)}, bf16[1,8,32,256]{3,2,1,0:T(8,128)(2,1)S(1)}, u32[]{:S(2)}, u32[]{:S(2)}) %collective-permute-start.13) | collective-permute-done | bytes 131104 | tf_op jit(solution)/shard_map/ppermute | solution.py:17
  69.3 1.2 %collective-permute-done.12 = bf16[1,8,32,256]{3,2,1,0:T(8,128)(2,1)S(1)} collective-permute-done((bf16[1,8,32,256]{3,2,1,0:T(8,128)(2,1)S(1)}, bf16[1,8,32,256]{3,2,1,0:T(8,128)(2,1)S(1)}, u32[]{:S(2)}, u32[]{:S(2)}) %collective-permute-start.12) | collective-permute-done | bytes 131104 | tf_op jit(solution)/shard_map/ppermute | solution.py:14
  70.5 1.3 %collective-permute-start.15 = (bf16[8,1,32,256]{3,2,1,0:T(8,128)(2,1)S(1)}, bf16[8,1,32,256]{3,2,1,0:T(8,128)(2,1)S(1)}, u32[]{:S(2)}, u32[]{:S(2)}) collective-permute-start(bf16[8,1,32,256]{3,2,1,0:T(8,128)(2,1)S(1)} %get-tuple-element.42), channel_id=1, source_target_pairs={{2,0},{3,1},{6,4},{7,5},{10,8},{11,9},{14,12},{15,13},{18,16},{19,... | collective-permute-start | bytes 393224 | tf_op jit(solution)/shard_map/ppermute | solution.py:17
  71.8 4.7 %collective-permute-start.14 = (bf16[8,1,32,256]{3,2,1,0:T(8,128)(2,1)S(1)}, bf16[8,1,32,256]{3,2,1,0:T(8,128)(2,1)S(1)}, u32[]{:S(2)}, u32[]{:S(2)}) collective-permute-start(bf16[8,1,32,256]{3,2,1,0:T(8,128)(2,1)S(1)} %get-tuple-element.41), channel_id=1, source_target_pairs={{0,2},{1,3},{4,6},{5,7},{8,10},{9,11},{12,14},{13,15},{16,18},{17,... | collective-permute-start | bytes 393224 | tf_op jit(solution)/shard_map/ppermute | solution.py:14
  76.5 1.6 %fusion.26 = (bf16[1,3,3,256,128]{4,3,2,1,0:T(8,128)(2,1)S(1)}, bf16[1,3,3,256,128]{4,3,2,1,0:T(8,128)(2,1)S(1)}, bf16[1,3,3,256,128]{4,3,2,1,0:T(8,128)(2,1)S(1)}) fusion(bf16[3,3,3,256,128]{4,3,2,1,0:T(8,128)(2,1)} %param.20), kind=kLoop, calls=%fused_computation.166 | loop fusion | bytes 3538944 | tf_op jit(solution)/shard_map/slice | solution.py:45
  79.0 1.3 %collective-permute-start.17 = (bf16[8,10,1,256]{3,2,1,0:T(2,128)(2,1)S(1)}, bf16[8,10,1,256]{3,2,1,0:T(2,128)(2,1)S(1)}, u32[]{:S(2)}, u32[]{:S(2)}) collective-permute-start(bf16[8,10,1,256]{3,2,1,0:T(2,128)(2,1)S(1)} %get-tuple-element.31), channel_id=1, source_target_pairs={{1,0},{3,2},{5,4},{7,6},{9,8},{11,10},{13,12},{15,14},{17,16},{19,... | collective-permute-start | bytes 122888 | tf_op jit(solution)/shard_map/ppermute | solution.py:17
  80.3 3.0 %collective-permute-start.16 = (bf16[8,10,1,256]{3,2,1,0:T(2,128)(2,1)S(1)}, bf16[8,10,1,256]{3,2,1,0:T(2,128)(2,1)S(1)}, u32[]{:S(2)}, u32[]{:S(2)}) collective-permute-start(bf16[8,10,1,256]{3,2,1,0:T(2,128)(2,1)S(1)} %get-tuple-element.32), channel_id=1, source_target_pairs={{0,1},{2,3},{4,5},{6,7},{8,9},{10,11},{12,13},{14,15},{16,17},{18,... | collective-permute-start | bytes 122888 | tf_op jit(solution)/shard_map/ppermute | solution.py:14
  84.2 2.5 %pad_maximum_fusion = (bf16[8,10,33,256]{3,2,1,0:T(8,128)(2,1)S(1)}, bf16[8,10,33,256]{3,2,1,0:T(8,128)(2,1)S(1)}) fusion(bf16[8,10,1,256]{3,2,1,0:T(2,128)(2,1)S(1)} %collective-permute-done.17, bf16[8,1,32,256]{3,2,1,0:T(8,128)(2,1)S(1)} %collective-permute-done.15, bf16[1,8,32,256]{3,2,1,0:T(8,128)(2,1)S(1)} %collective-permute-done.13, ...), kind=kLoop, calls=%fused_computation.7 | loop fusion | flops 18923520 | bytes 4096000 | tf_op jit(solution)/shard_map/concatenate | solution.py:18
  90.4 2.0 %fusion.33 = f32[1536,128]{1,0:T(8,128)S(1)} fusion(bf16[1536,2304]{1,0:T(8,128)(2,1)S(1)} %bitcast.125, bf16[2304,128]{1,0:T(8,128)(2,1)S(1)} %bitcast.114), kind=kOutput, calls=%fused_computation.173 | convolution fusion | flops 905969664 | bytes 8454144 | tf_op jit(solution)/shard_map/dot_general | solution.py:43
  92.7 2.1 %convolution_add_fusion.3 = f32[1536,128]{1,0:T(8,128)S(1)} fusion(f32[1536,128]{1,0:T(8,128)S(1)} %fusion.33, bf16[1536,2304]{1,0:T(8,128)(2,1)S(1)} %constant_dynamic-update-slice_fusion.31, bf16[2304,128]{1,0:T(8,128)(2,1)S(1)} %bitcast.106), kind=kOutput, calls=%fused_computation.4 | convolution fusion | flops 906166272 | bytes 9240576 | tf_op jit(solution)/shard_map/dot_general | solution.py:43
  94.9 2.8 %fusion.3 = bf16[1536,128]{1,0:T(8,128)(2,1)} fusion(f32[1536,128]{1,0:T(8,128)S(1)} %convolution_add_fusion.3, bf16[1536,2304]{1,0:T(8,128)(2,1)S(1)} %bitcast.124, bf16[2304,128]{1,0:T(8,128)(2,1)S(1)} %bitcast.113, f32[128]{0:T(128)S(1)} %copy-done.9), kind=kOutput, calls=%fused_computation.11 | convolution fusion | flops 906952704 | bytes 8847872 | tf_op jit(solution)/shard_map/dot_general | solution.py:43
  (106 shorter events, 19.3 us)
Async XLA Ops:
  0.0 33.8 %copy-start = (bf16[2,2,2,128,256]{4,3,2,1,0:T(8,128)(2,1)S(1)}, bf16[2,2,2,128,256]{4,3,2,1,0:T(8,128)(2,1)}, u32[]{:S(2)}) copy-start(bf16[2,2,2,128,256]{4,3,2,1,0:T(8,128)(2,1)} %param.14) | copy-start | bytes 1572868
  0.9 6.8 %collective-permute-start = (bf16[1,8,32,128]{3,2,1,0:T(8,128)(2,1)S(1)}, bf16[1,8,32,128]{3,2,1,0:T(8,128)(2,1)S(1)}, u32[]{:S(2)}, u32[]{:S(2)}) collective-permute-start(bf16[1,8,32,128]{3,2,1,0:T(8,128)(2,1)S(1)} %get-tuple-element.84), channel_id=1, source_target_pairs={{0,4},{4,8},{8,12},{1,5},{5,9},{9,13},{2,6},{6,10},{10,14},{3,7},{... | collective-permute-start | bytes 196616 | tf_op jit(solution)/shard_map/ppermute | solution.py:14
  5.9 6.2 %collective-permute-start.1 = (bf16[1,8,32,128]{3,2,1,0:T(8,128)(2,1)S(1)}, bf16[1,8,32,128]{3,2,1,0:T(8,128)(2,1)S(1)}, u32[]{:S(2)}, u32[]{:S(2)}) collective-permute-start(bf16[1,8,32,128]{3,2,1,0:T(8,128)(2,1)S(1)} %get-tuple-element.83), channel_id=1, source_target_pairs={{4,0},{8,4},{12,8},{5,1},{9,5},{13,9},{6,2},{10,6},{14,10},{7,3},{... | collective-permute-start | bytes 196616 | tf_op jit(solution)/shard_map/ppermute | solution.py:17
  12.1 6.2 %collective-permute-start.3 = (bf16[8,1,32,128]{3,2,1,0:T(8,128)(2,1)S(1)}, bf16[8,1,32,128]{3,2,1,0:T(8,128)(2,1)S(1)}, u32[]{:S(2)}, u32[]{:S(2)}) collective-permute-start(bf16[8,1,32,128]{3,2,1,0:T(8,128)(2,1)S(1)} %get-tuple-element.79), channel_id=1, source_target_pairs={{2,0},{3,1},{6,4},{7,5},{10,8},{11,9},{14,12},{15,13},{18,16},{19,... | collective-permute-start | bytes 196616 | tf_op jit(solution)/shard_map/ppermute | solution.py:17
  13.4 6.4 %collective-permute-start.2 = (bf16[8,1,32,128]{3,2,1,0:T(8,128)(2,1)S(1)}, bf16[8,1,32,128]{3,2,1,0:T(8,128)(2,1)S(1)}, u32[]{:S(2)}, u32[]{:S(2)}) collective-permute-start(bf16[8,1,32,128]{3,2,1,0:T(8,128)(2,1)S(1)} %get-tuple-element.78), channel_id=1, source_target_pairs={{0,2},{1,3},{4,6},{5,7},{8,10},{9,11},{12,14},{13,15},{16,18},{17,... | collective-permute-start | bytes 196616 | tf_op jit(solution)/shard_map/ppermute | solution.py:14
  19.9 5.6 %collective-permute-start.5 = (bf16[8,10,1,128]{3,2,1,0:T(2,128)(2,1)S(1)}, bf16[8,10,1,128]{3,2,1,0:T(2,128)(2,1)S(1)}, u32[]{:S(2)}, u32[]{:S(2)}) collective-permute-start(bf16[8,10,1,128]{3,2,1,0:T(2,128)(2,1)S(1)} %get-tuple-element.70), channel_id=1, source_target_pairs={{1,0},{3,2},{5,4},{7,6},{9,8},{11,10},{13,12},{15,14},{17,16},{19,... | collective-permute-start | bytes 61448 | tf_op jit(solution)/shard_map/ppermute | solution.py:17
  21.2 4.3 %collective-permute-start.4 = (bf16[8,10,1,128]{3,2,1,0:T(2,128)(2,1)S(1)}, bf16[8,10,1,128]{3,2,1,0:T(2,128)(2,1)S(1)}, u32[]{:S(2)}, u32[]{:S(2)}) collective-permute-start(bf16[8,10,1,128]{3,2,1,0:T(2,128)(2,1)S(1)} %get-tuple-element.71), channel_id=1, source_target_pairs={{0,1},{2,3},{4,5},{6,7},{8,9},{10,11},{12,13},{14,15},{16,17},{18,... | collective-permute-start | bytes 61448 | tf_op jit(solution)/shard_map/ppermute | solution.py:14
  26.3 1.3 %copy-start.2 = (bf16[6,8,32,128]{3,2,1,0:T(8,128)(2,1)S(1)}, bf16[6,8,32,128]{3,2,1,0:T(8,128)(2,1)}, u32[]{:S(2)}) copy-start(bf16[6,8,32,128]{3,2,1,0:T(8,128)(2,1)} %param.11) | copy-start | bytes 1179652
  30.9 1.1 %copy-start.8 = (f32[128]{0:T(128)S(1)}, f32[128]{0:T(128)}, u32[]{:S(2)}) copy-start(f32[128]{0:T(128)} %param.13) | copy-start | bytes 1540
  32.1 1.7 %copy-start.5 = (f32[256]{0:T(256)S(1)}, f32[256]{0:T(256)}, u32[]{:S(2)}) copy-start(f32[256]{0:T(256)} %param.15) | copy-start | bytes 3076
  34.1 9.2 %collective-permute-start.7 = (bf16[1,4,16,256]{3,2,1,0:T(8,128)(2,1)S(1)}, bf16[1,4,16,256]{3,2,1,0:T(8,128)(2,1)S(1)}, u32[]{:S(2)}, u32[]{:S(2)}) collective-permute-start(bf16[1,4,16,256]{3,2,1,0:T(8,128)(2,1)S(1)} %bitcast.128), channel_id=1, source_target_pairs={{4,0},{8,4},{12,8},{5,1},{9,5},{13,9},{6,2},{10,6},{14,10},{7,3},{... | collective-permute-start | bytes 98312 | tf_op jit(solution)/shard_map/ppermute | solution.py:17
  35.4 13.8 %copy-start.7 = (f32[128]{0:T(128)S(1)}, f32[128]{0:T(128)}, u32[]{:S(2)}) copy-start(f32[128]{0:T(128)} %param.19) | copy-start | bytes 1540
  35.4 7.9 %collective-permute-start.6 = (bf16[1,4,16,256]{3,2,1,0:T(8,128)(2,1)S(1)}, bf16[1,4,16,256]{3,2,1,0:T(8,128)(2,1)S(1)}, u32[]{:S(2)}, u32[]{:S(2)}) collective-permute-start(bf16[1,4,16,256]{3,2,1,0:T(8,128)(2,1)S(1)} %bitcast.127), channel_id=1, source_target_pairs={{0,4},{4,8},{8,12},{1,5},{5,9},{9,13},{2,6},{6,10},{10,14},{3,7},{... | collective-permute-start | bytes 98312 | tf_op jit(solution)/shard_map/ppermute | solution.py:14
  43.4 7.9 %collective-permute-start.9 = (bf16[5,1,16,256]{3,2,1,0:T(8,128)(2,1)S(1)}, bf16[5,1,16,256]{3,2,1,0:T(8,128)(2,1)S(1)}, u32[]{:S(2)}, u32[]{:S(2)}) collective-permute-start(bf16[5,1,16,256]{3,2,1,0:T(8,128)(2,1)S(1)} %get-tuple-element.116), channel_id=1, source_target_pairs={{2,0},{3,1},{6,4},{7,5},{10,8},{11,9},{14,12},{15,13},{18,16},{19,... | collective-permute-start | bytes 122888 | tf_op jit(solution)/shard_map/ppermute | solution.py:17
  44.7 6.6 %collective-permute-start.8 = (bf16[5,1,16,256]{3,2,1,0:T(8,128)(2,1)S(1)}, bf16[5,1,16,256]{3,2,1,0:T(8,128)(2,1)S(1)}, u32[]{:S(2)}, u32[]{:S(2)}) collective-permute-start(bf16[5,1,16,256]{3,2,1,0:T(8,128)(2,1)S(1)} %get-tuple-element.115), channel_id=1, source_target_pairs={{0,2},{1,3},{4,6},{5,7},{8,10},{9,11},{12,14},{13,15},{16,18},{17,... | collective-permute-start | bytes 122888 | tf_op jit(solution)/shard_map/ppermute | solution.py:14
  51.3 4.4 %collective-permute-start.11 = (bf16[5,6,1,256]{3,2,1,0:T(2,128)(2,1)S(1)}, bf16[5,6,1,256]{3,2,1,0:T(2,128)(2,1)S(1)}, u32[]{:S(2)}, u32[]{:S(2)}) collective-permute-start(bf16[5,6,1,256]{3,2,1,0:T(2,128)(2,1)S(1)} %get-tuple-element.105), channel_id=1, source_target_pairs={{1,0},{3,2},{5,4},{7,6},{9,8},{11,10},{13,12},{15,14},{17,16},{19,... | collective-permute-start | bytes 46088 | tf_op jit(solution)/shard_map/ppermute | solution.py:17
  52.6 3.9 %collective-permute-start.10 = (bf16[5,6,1,256]{3,2,1,0:T(2,128)(2,1)S(1)}, bf16[5,6,1,256]{3,2,1,0:T(2,128)(2,1)S(1)}, u32[]{:S(2)}, u32[]{:S(2)}) collective-permute-start(bf16[5,6,1,256]{3,2,1,0:T(2,128)(2,1)S(1)} %get-tuple-element.106), channel_id=1, source_target_pairs={{0,1},{2,3},{4,5},{6,7},{8,9},{10,11},{12,13},{14,15},{16,17},{18,... | collective-permute-start | bytes 46088 | tf_op jit(solution)/shard_map/ppermute | solution.py:14
  57.0 1.1 %copy-start.6 = (f32[256]{0:T(256)S(1)}, f32[256]{0:T(256)}, u32[]{:S(2)}) copy-start(f32[256]{0:T(256)} %param.17) | copy-start | bytes 3076
  57.1 1.0 %copy-start.4 = (bf16[3,4,16,2304]{3,2,1,0:T(8,128)(2,1)}, bf16[3,4,16,2304]{3,2,1,0:T(8,128)(2,1)S(1)}, u32[]{:S(2)}) copy-start(bf16[3,4,16,2304]{3,2,1,0:T(8,128)(2,1)S(1)} %get-tuple-element.85) | copy-start | bytes 2654212
  57.1 1.4 %copy-start.3 = (bf16[2,2,2,256,128]{3,4,2,1,0:T(8,128)(2,1)S(1)}, bf16[2,2,2,256,128]{3,4,2,1,0:T(8,128)(2,1)}, u32[]{:S(2)}) copy-start(bf16[2,2,2,256,128]{3,4,2,1,0:T(8,128)(2,1)} %copy.14) | copy-start | bytes 1572868
  61.6 7.6 %collective-permute-start.13 = (bf16[1,8,32,256]{3,2,1,0:T(8,128)(2,1)S(1)}, bf16[1,8,32,256]{3,2,1,0:T(8,128)(2,1)S(1)}, u32[]{:S(2)}, u32[]{:S(2)}) collective-permute-start(bf16[1,8,32,256]{3,2,1,0:T(8,128)(2,1)S(1)} %get-tuple-element.67), channel_id=1, source_target_pairs={{4,0},{8,4},{12,8},{5,1},{9,5},{13,9},{6,2},{10,6},{14,10},{7,3},{... | collective-permute-start | bytes 393224 | tf_op jit(solution)/shard_map/ppermute | solution.py:17
  62.9 7.5 %collective-permute-start.12 = (bf16[1,8,32,256]{3,2,1,0:T(8,128)(2,1)S(1)}, bf16[1,8,32,256]{3,2,1,0:T(8,128)(2,1)S(1)}, u32[]{:S(2)}, u32[]{:S(2)}) collective-permute-start(bf16[1,8,32,256]{3,2,1,0:T(8,128)(2,1)S(1)} %get-tuple-element.66), channel_id=1, source_target_pairs={{0,4},{4,8},{8,12},{1,5},{5,9},{9,13},{2,6},{6,10},{10,14},{3,7},{... | collective-permute-start | bytes 393224 | tf_op jit(solution)/shard_map/ppermute | solution.py:14
  70.5 7.6 %collective-permute-start.15 = (bf16[8,1,32,256]{3,2,1,0:T(8,128)(2,1)S(1)}, bf16[8,1,32,256]{3,2,1,0:T(8,128)(2,1)S(1)}, u32[]{:S(2)}, u32[]{:S(2)}) collective-permute-start(bf16[8,1,32,256]{3,2,1,0:T(8,128)(2,1)S(1)} %get-tuple-element.42), channel_id=1, source_target_pairs={{2,0},{3,1},{6,4},{7,5},{10,8},{11,9},{14,12},{15,13},{18,16},{19,... | collective-permute-start | bytes 393224 | tf_op jit(solution)/shard_map/ppermute | solution.py:17
  71.8 7.1 %collective-permute-start.14 = (bf16[8,1,32,256]{3,2,1,0:T(8,128)(2,1)S(1)}, bf16[8,1,32,256]{3,2,1,0:T(8,128)(2,1)S(1)}, u32[]{:S(2)}, u32[]{:S(2)}) collective-permute-start(bf16[8,1,32,256]{3,2,1,0:T(8,128)(2,1)S(1)} %get-tuple-element.41), channel_id=1, source_target_pairs={{0,2},{1,3},{4,6},{5,7},{8,10},{9,11},{12,14},{13,15},{16,18},{17,... | collective-permute-start | bytes 393224 | tf_op jit(solution)/shard_map/ppermute | solution.py:14
  79.0 4.7 %collective-permute-start.17 = (bf16[8,10,1,256]{3,2,1,0:T(2,128)(2,1)S(1)}, bf16[8,10,1,256]{3,2,1,0:T(2,128)(2,1)S(1)}, u32[]{:S(2)}, u32[]{:S(2)}) collective-permute-start(bf16[8,10,1,256]{3,2,1,0:T(2,128)(2,1)S(1)} %get-tuple-element.31), channel_id=1, source_target_pairs={{1,0},{3,2},{5,4},{7,6},{9,8},{11,10},{13,12},{15,14},{17,16},{19,... | collective-permute-start | bytes 122888 | tf_op jit(solution)/shard_map/ppermute | solution.py:17
  80.3 3.9 %collective-permute-start.16 = (bf16[8,10,1,256]{3,2,1,0:T(2,128)(2,1)S(1)}, bf16[8,10,1,256]{3,2,1,0:T(2,128)(2,1)S(1)}, u32[]{:S(2)}, u32[]{:S(2)}) collective-permute-start(bf16[8,10,1,256]{3,2,1,0:T(2,128)(2,1)S(1)} %get-tuple-element.32), channel_id=1, source_target_pairs={{0,1},{2,3},{4,5},{6,7},{8,9},{10,11},{12,13},{14,15},{16,17},{18,... | collective-permute-start | bytes 122888 | tf_op jit(solution)/shard_map/ppermute | solution.py:14
  92.7 2.1 %copy-start.9 = (f32[128]{0:T(128)S(1)}, f32[128]{0:T(128)}, u32[]{:S(2)}) copy-start(f32[128]{0:T(128)} %param.21) | copy-start | bytes 1540
  94.8 2.8 %copy-start.1 = (bf16[2,2,2,128,256]{4,3,2,1,0:T(8,128)(2,1)S(1)}, bf16[2,2,2,128,256]{4,3,2,1,0:T(8,128)(2,1)}, u32[]{:S(2)}) copy-start(bf16[2,2,2,128,256]{4,3,2,1,0:T(8,128)(2,1)} %param.14) | copy-start | bytes 1572868
where the time goes:
time: 99.3 us; the launch traced here: 97.7 us
  starting transfers between devices  48.6 us (49%)
  local copies, waits for them, and re-layouts  18.3 us (18%)
  matrix products  13.7 us (14%)
  waiting for transfers between devices  10.7 us (11%)
  other arithmetic  5.5 us (6%)
    ppermute x9, starting transfers between devices, padded_2(): lax.ppermute(lax.slice_in_dim(block, block.shape[dim] - width, None, axis...  37 us
    ppermute x9, starting transfers between devices, padded_2(): lax.ppermute(lax.slice_in_dim(block, 0, width, axis=dim), axis, backward)  11.6 us
    dot_general x8, matrix products, conv_taps(): jnp.dot(window_rows.reshape(-1, 9 * channels), weight[offset_a].reshape(9...  11.1 us
    unnamed x59, local copies, waits for them, and re-layouts  8.53 us
    slice x3, local copies, waits for them, and re-layouts, conv_taps(): weight[offset_a].reshape(9 * channels, outputs)  6.15 us
    ppermute x9, waiting for transfers between devices, padded_2(): lax.ppermute(lax.slice_in_dim(block, block.shape[dim] - width, None, axis...  5.35 us
    ppermute x9, waiting for transfers between devices, padded_2(): lax.ppermute(lax.slice_in_dim(block, 0, width, axis=dim), axis, backward)  5.31 us
    concatenate x8, other arithmetic, padded_2(): block = jnp.concatenate([low, block, high], axis=dim)  3.95 us
  transfers between devices with their start and end apart: 18, of which 9 were waited for; matrix products, arithmetic and copies ran while one was open for 10% of the time, Pallas kernels for 0%

commit v1 on v0

v1 whole, which is shorter than its diff:
```python
import functools
import itertools

import jax
import jax.numpy as jnp
from jax import lax
from jax.experimental import pallas as pl
from jax.experimental.pallas import tpu as pltpu
from jax.sharding import PartitionSpec as P

leak_slope = 0.01
MESH = pl.DeviceIdType.MESH
lead = 8
plane_steps = [s for s in itertools.product((-1, 0, 1), repeat=2) if s != (0, 0)]
width_steps = (-1, 1)


def leaky_relu(values):
    return jnp.maximum(values, leak_slope * values)


def rounded(values):
    return values.astype(jnp.bfloat16)


def source_span(step, cells, base):
    if step == 0:
        return pl.ds(base, cells)
    return pl.ds(base + (0 if step < 0 else cells - 1), 1)


def target_span(step, cells):
    if step == 0:
        return pl.ds(1, cells)
    return pl.ds(cells + 1 if step < 0 else 0, 1)


def kernel(
    sizes,
    volume,
    w_encode,
    w_down,
    w_bottom,
    w_up,
    w_decode,
    b_encode_far,
    b_down_far,
    b_bottom_far,
    b_up_far,
    b_decode_far,
    decoded,
    v_cells,
    e_cells,
    r_cells,
    c_cells,
    v_frame,
    e_frame,
    r_frame,
    c_frame,
    v_taps,
    e_taps,
    r_taps,
    c_taps,
    edge_out,
    edge_in,
    c_edge_out,
    c_edge_in,
    encode_pairs,
    skip_pairs,
    raised_pairs,
    down_matrix,
    bottom_matrix,
    up_matrix,
    down_rows,
    partial,
    result,
    b_encode,
    b_down,
    b_bottom,
    b_up,
    b_decode,
    send_sem,
    recv_sem,
    edge_send_sem,
    edge_recv_sem,
    load_sem,
    store_sem,
):
    depth, height, width, skip = volume.shape
    half_depth, half_height, half_width = depth // 2, height // 2, width // 2
    deep = w_down.shape[-1]
    deep_size, high_size, wide_size = sizes
    at_deep, at_high, at_wide = (lax.axis_index(name) for name in ("wide", "narrow", "pair"))

    def inside(place, step, size):
        return jnp.logical_and(place + step >= 0, place + step < size)

    def plane_exists(step):
        return jnp.logical_and(
            inside(at_deep, step[0], deep_size), inside(at_high, step[1], high_size)
        )

    def width_exists(step):
        return inside(at_wide, step, wide_size)

    plane_used = [
        s
        for s in plane_steps
        if (s[0] == 0 or deep_size > 1) and (s[1] == 0 or high_size > 1)
    ]
    width_used = width_steps if wide_size > 1 else ()

    loads = []

    def load(source, target):
        copy = pltpu.make_async_copy(source, target, load_sem.at[len(loads)])
        copy.start()
        loads.append(copy)
        return copy

    own_load = load(volume, v_cells.at[pl.ds(1, depth), pl.ds(1, height)])

    def load_pairs(weight, first, target):
        return [
            load(
                weight.at[a, :, :, pl.ds(first, skip), :],
                target.at[a, pl.ds(j, 3), :, :, pl.ds(j * skip, skip)],
            )
            for a in range(3)
            for j in range(2)
        ]

    encode_loads = load_pairs(w_encode, 0, encode_pairs)
    encode_loads += [
        load(b_encode_far, b_encode),
        load(b_down_far, b_down),
        load(b_bottom_far, b_bottom),
        load(b_up_far, b_up),
        load(b_decode_far, b_decode),
    ]
    down_load = load(w_down, down_matrix)

    def zero_halo(cells, planes, rows):
        blank = jnp.zeros(cells.shape[2:], cells.dtype)
        for z in range(planes + 2):
            for y in range(rows + 2):
                if z in (0, planes + 1) or y in (0, rows + 1):
                    cells[z, y] = blank

    for cells in (v_cells, e_cells, r_cells):
        zero_halo(cells, depth, height)
    zero_halo(c_cells, half_depth, half_height)
    edge_in[...] = jnp.zeros_like(edge_in)
    c_edge_in[...] = jnp.zeros_like(c_edge_in)

    barrier = pltpu.get_barrier_semaphore()
    for step in plane_used:

        @pl.when(plane_exists(step))
        def _():
            pl.semaphore_signal(
                barrier,
                inc=1,
                device_id={"wide": at_deep + step[0], "narrow": at_high + step[1]},
                device_id_type=MESH,
            )

    for step in width_used:

        @pl.when(width_exists(step))
        def _():
            pl.semaphore_signal(
                barrier, inc=1, device_id={"pair": at_wide + step}, device_id_type=MESH
            )

    peers = sum(
        [plane_exists(step).astype(jnp.int32) for step in plane_used]
        + [width_exists(step).astype(jnp.int32) for step in width_used]
    )
    pl.semaphore_wait(barrier, peers)

    started = []

    def send_planes(slot, cells, source, base, planes, rows):
        copies = []
        for k, step in enumerate(plane_used):
            copy = pltpu.make_async_remote_copy(
                src_ref=source.at[
                    source_span(step[0], planes, base), source_span(step[1], rows, base)
                ],
                dst_ref=cells.at[target_span(step[0], planes), target_span(step[1], rows)],
                send_sem=send_sem.at[slot, k],
                recv_sem=recv_sem.at[slot, k],
                device_id={"wide": at_deep + step[0], "narrow": at_high + step[1]},
                device_id_type=MESH,
            )
            pl.when(plane_exists(step))(copy.start)
            copies.append((plane_exists((-step[0], -step[1])), copy))
            started.append((plane_exists(step), copy))
        return copies

    def send_edges(slot, out, arriving):
        copies = []
        for k, step in enumerate(width_used):
            copy = pltpu.make_async_remote_copy(
                src_ref=out.at[k],
                dst_ref=arriving.at[k],
                send_sem=edge_send_sem.at[slot, k],
                recv_sem=edge_recv_sem.at[slot, k],
                device_id={"pair": at_wide + step},
                device_id_type=MESH,
            )
            pl.when(width_exists(step))(copy.start)
            copies.append((width_exists(-step), copy))
            started.append((width_exists(step), copy))
        return copies

    def arrive(copies):
        for exists, copy in copies:
            pl.when(exists)(copy.wait_recv)

    def take_edges(frame, out, cells):
        count, pitch, channels = frame.shape
        flat = frame.reshape(count * pitch, channels)
        out[0] = rounded(flat[pl.ds(lead, count, stride=pitch), :])
        out[1] = rounded(flat[pl.ds(lead + cells - 1, count, stride=pitch), :])

    def lanes(h):
        return pl.ds(h * skip, skip)

    def put_edges(frame, arriving, cells):
        count, pitch, channels = frame.shape
        flat = frame.reshape(count * pitch, channels)
        flat[pl.ds(lead + cells, count, stride=pitch), :] = arriving[0].astype(jnp.float32)
        flat[pl.ds(lead - 1, count, stride=pitch), :] = arriving[1].astype(jnp.float32)

    def halo_to_frame(cells, frame, planes, rows, span):
        for z in range(planes + 2):
            for y in range(rows + 2):
                if z in (0, planes + 1) or y in (0, rows + 1):
                    frame[z * (rows + 2) + y, lead : lead + span, :] = cells[z, y].astype(
                        jnp.float32
                    )

    deep_parts = range(deep // skip)

    def spread_taps(frame, taps):
        def one(z, carry):
            for y in range(height + 2):
                for c in range(3):
                    taps[z, y // 2, y % 2, :, c * skip : (c + 1) * skip] = rounded(
                        frame[z * (height + 2) + y, lead - 1 + c : lead - 1 + c + width, :]
                    )
            return carry

        lax.fori_loop(0, depth + 2, one, 0)

    def pair_conv(taps, matrix, z):
        total = None
        for a in range(3):
            rows = jnp.concatenate(
                [
                    taps[pl.ds(z + a, 2), pl.ds(r // 2, half_height), r % 2].reshape(
                        2 * half_height * width, 3 * skip
                    )
                    for r in range(4)
                ],
                axis=-1,
            )
            term = jnp.dot(
                rows,
                matrix[a].reshape(12 * skip, 2 * skip),
                preferred_element_type=jnp.float32,
            )
            total = term if total is None else total + term
        return total

    v_copies = send_planes(0, v_cells, volume, 0, depth, height)
    bottom_load = load(w_bottom, bottom_matrix)
    skip_loads = load_pairs(w_decode, skip, skip_pairs)
    up_loads = [
        load(
            w_up.at[a, b, c],
            up_matrix.at[:, pl.ds(((a * 2 + b) * 2 + c) * skip, skip)],
        )
        for a, b, c in itertools.product((0, 1), repeat=3)
    ]
    raised_loads = load_pairs(w_decode, 0, raised_pairs)
    for pairs in (encode_pairs, skip_pairs, raised_pairs):
        for a in range(3):
            pairs[a, 0, :, :, skip : 2 * skip] = jnp.zeros((3, skip, skip), jnp.bfloat16)
            pairs[a, 3, :, :, 0:skip] = jnp.zeros((3, skip, skip), jnp.bfloat16)
    c_frame[...] = jnp.zeros_like(c_frame)
    own_load.wait()
    arrive(v_copies)

    def widen(z, carry):
        for y in range(height + 2):
            v_frame[z * (height + 2) + y, lead : lead + width, :] = v_cells[z, y].astype(
                jnp.float32
            )
        return carry

    lax.fori_loop(0, depth + 2, widen, 0)
    take_edges(v_frame, edge_out.at[0], width)
    v_edges = send_edges(0, edge_out.at[0], edge_in.at[0])
    for copy in encode_loads:
        copy.wait()
    arrive(v_edges)
    put_edges(v_frame, edge_in.at[0], width)
    spread_taps(v_frame, v_taps)
    encode_bias = jnp.concatenate([b_encode[...], b_encode[...]], axis=-1)

    def encode(i, carry):
        z = 2 * i
        values = rounded(leaky_relu(pair_conv(v_taps, encode_pairs, z) + encode_bias))
        values = values.reshape(2, half_height, width, 2 * skip)
        for dz in range(2):
            for y in range(height):
                cells = values[dz, y // 2, :, (y % 2) * skip : (y % 2 + 1) * skip]
                e_cells[z + dz + 1, y + 1] = cells
                e_frame[
                    (z + dz + 1) * (height + 2) + y + 1, lead : lead + width, :
                ] = cells.astype(jnp.float32)
        return carry

    lax.fori_loop(0, half_depth, encode, 0)
    e_copies = send_planes(1, e_cells, e_cells, 1, depth, height)

    def gather_down(z, carry):
        for y in range(half_height):
            for a, b, c in itertools.product((0, 1), repeat=3):
                tap = (a * 2 + b) * 2 + c
                down_rows[z, y, :, tap * skip : (tap + 1) * skip] = rounded(
                    e_frame[
                        (2 * z + a + 1) * (height + 2) + 2 * y + b + 1,
                        pl.ds(lead + c, half_width, stride=2),
                        :,
                    ]
                )
        return carry

    lax.fori_loop(0, half_depth, gather_down, 0)
    down_load.wait()
    low_cells = half_depth * half_height * half_width
    coarse = jnp.dot(
        down_rows[...].reshape(low_cells, 8 * skip),
        down_matrix[...].reshape(8 * skip, deep),
        preferred_element_type=jnp.float32,
    )
    coarse = rounded(leaky_relu(coarse + b_down[...]))
    coarse = coarse.reshape(half_depth, half_height, half_width, deep)
    c_cells[1 : 1 + half_depth, 1 : 1 + half_height] = coarse
    c_copies = send_planes(2, c_cells, c_cells, 1, half_depth, half_height)
    for z in range(half_depth):
        for y in range(half_height):
            for h in deep_parts:
                c_frame[
                    h, (z + 1) * (half_height + 2) + y + 1, lead : lead + half_width, :
                ] = coarse[z, y, :, h * skip : (h + 1) * skip].astype(jnp.float32)

    arrive(e_copies)
    halo_to_frame(e_cells, e_frame, depth, height, width)
    take_edges(e_frame, edge_out.at[1], width)
    e_edges = send_edges(1, edge_out.at[1], edge_in.at[1])

    arrive(c_copies)
    for h in deep_parts:
        part = c_cells.at[:, :, :, lanes(h)]
        halo_to_frame(part, c_frame.at[h], half_depth, half_height, half_width)
        take_edges(c_frame.at[h], c_edge_out.at[:, :, lanes(h)], half_width)
    c_edges = send_edges(2, c_edge_out, c_edge_in)

    arrive(e_edges)
    put_edges(e_frame, edge_in.at[1], width)
    spread_taps(e_frame, e_taps)
    for copy in skip_loads:
        copy.wait()

    def decode_skip(i):
        partial[i] = pair_conv(e_taps, skip_pairs, 2 * i)

    decode_skip(0)

    arrive(c_edges)
    for h in deep_parts:
        put_edges(c_frame.at[h], c_edge_in.at[:, :, lanes(h)], half_width)
    for z in range(half_depth + 2):
        for y in range(half_height + 2):
            for c, h in itertools.product(range(3), deep_parts):
                first = c * deep + h * skip
                c_taps[z, y, :, first : first + skip] = rounded(
                    c_frame[
                        h, z * (half_height + 2) + y, lead - 1 + c : lead - 1 + c + half_width, :
                    ]
                )
    bottom_load.wait()
    total = jnp.zeros((low_cells, deep), jnp.float32)
    for a in range(3):
        for b in range(3):
            total += jnp.dot(
                c_taps[a : a + half_depth, b : b + half_height].reshape(low_cells, 3 * deep),
                bottom_matrix[a, b].reshape(3 * deep, deep),
                preferred_element_type=jnp.float32,
            )
    bottom = rounded(leaky_relu(total + b_bottom[...]))
    for copy in up_loads:
        copy.wait()
    up_bias = jnp.concatenate([b_up[...], b_up[...]], axis=-1)
    for a in range(2):
        for b in range(2):
            first = (a * 2 + b) * 2 * skip
            lifted = jnp.dot(
                bottom, up_matrix[:, first : first + 2 * skip], preferred_element_type=jnp.float32
            )
            lifted = rounded(lifted + up_bias).astype(jnp.float32)
            lifted = lifted.reshape(half_depth, half_height, half_width, 2 * skip)
            for z in range(half_depth):
                for y in range(half_height):
                    plane = (2 * z + a + 1) * (height + 2) + 2 * y + b + 1
                    for c in range(2):
                        r_frame[plane, pl.ds(lead + c, half_width, stride=2), :] = lifted[
                            z, y, :, c * skip : (c + 1) * skip
                        ]

    def narrow_raised(z, carry):
        for y in range(height):
            r_cells[z + 1, y + 1] = rounded(
                r_frame[(z + 1) * (height + 2) + y + 1, lead : lead + width, :]
            )
        return carry

    lax.fori_loop(0, depth, narrow_raised, 0)
    r_copies = send_planes(3, r_cells, r_cells, 1, depth, height)

    chunks = list(range(1, half_depth))
    for i in chunks[: len(chunks) // 2]:
        decode_skip(i)
    arrive(r_copies)
    halo_to_frame(r_cells, r_frame, depth, height, width)
    take_edges(r_frame, edge_out.at[2], width)
    r_edges = send_edges(3, edge_out.at[2], edge_in.at[2])
    for i in chunks[len(chunks) // 2 :]:
        decode_skip(i)
    arrive(r_edges)
    put_edges(r_frame, edge_in.at[2], width)
    spread_taps(r_frame, r_taps)
    for copy in raised_loads:
        copy.wait()
    decode_bias = jnp.concatenate([b_decode[...], b_decode[...]], axis=-1)
    stores = []
    for i in range(half_depth):
        values = pair_conv(r_taps, raised_pairs, 2 * i) + partial[i]
        values = rounded(leaky_relu(values + decode_bias))
        values = values.reshape(2, half_height, width, 2 * skip)
        for dz in range(2):
            for y in range(height):
                result[2 * i + dz, y] = values[
                    dz, y // 2, :, (y % 2) * skip : (y % 2 + 1) * skip
                ]
        store = pltpu.make_async_copy(
            result.at[pl.ds(2 * i, 2)], decoded.at[pl.ds(2 * i, 2)], store_sem.at[i]
        )
        store.start()
        stores.append(store)
    for exists, copy in started:
        pl.when(exists)(copy.wait_send)
    for store in stores:
        store.wait()


def body(
    sizes,
    volume,
    w_encode,
    b_encode,
    w_down,
    b_down,
    w_bottom,
    b_bottom,
    w_up,
    b_up,
    w_decode,
    b_decode,
):
    depth, height, width, skip = volume.shape
    deep = w_down.shape[-1]
    half_depth, half_height, half_width = depth // 2, height // 2, width // 2
    planes = (depth + 2) * (height + 2)
    planes += -planes % 16
    low_planes = (half_depth + 2) * (half_height + 2)
    low_planes += -low_planes % 16
    half = jnp.bfloat16
    cells = pltpu.VMEM((depth + 2, height + 2, width, skip), half)
    frame = pltpu.VMEM((planes, width + 2 * lead, skip), jnp.float32)
    taps = pltpu.VMEM((depth + 2, height // 2 + 1, 2, width, 3 * skip), half)
    pairs = pltpu.VMEM((3, 4, 3, skip, 2 * skip), half)
    far = pl.BlockSpec(memory_space=pltpu.HBM)
    bias = lambda size: pltpu.VMEM((1, size), jnp.float32)
    return pl.pallas_call(
        functools.partial(kernel, sizes),
        out_shape=jax.ShapeDtypeStruct(volume.shape, half),
        in_specs=[far] * 11,
        out_specs=far,
        scratch_shapes=[
            cells,
            cells,
            cells,
            pltpu.VMEM((half_depth + 2, half_height + 2, half_width, deep), half),
            frame,
            frame,
            frame,
            pltpu.VMEM((deep // skip, low_planes, half_width + 2 * lead, skip), jnp.float32),
            taps,
            taps,
            taps,
            pltpu.VMEM((half_depth + 2, half_height + 2, half_width, 3 * deep), half),
            pltpu.VMEM((3, 2, planes, skip), half),
            pltpu.VMEM((3, 2, planes, skip), half),
            pltpu.VMEM((2, low_planes, deep), half),
            pltpu.VMEM((2, low_planes, deep), half),
            pairs,
            pairs,
            pairs,
            pltpu.VMEM(w_down.shape, half),
            pltpu.VMEM(w_bottom.shape, half),
            pltpu.VMEM((deep, 8 * skip), half),
            pltpu.VMEM((half_depth, half_height, half_width, 8 * skip), half),
            pltpu.VMEM((half_depth, height * width, 2 * skip), jnp.float32),
            pltpu.VMEM(volume.shape, half),
            bias(skip),
            bias(deep),
            bias(deep),
            bias(skip),
            bias(skip),
            pltpu.SemaphoreType.DMA((4, 8)),
            pltpu.SemaphoreType.DMA((4, 8)),
            pltpu.SemaphoreType.DMA((4, 2)),
            pltpu.SemaphoreType.DMA((4, 2)),
            pltpu.SemaphoreType.DMA((34,)),
            pltpu.SemaphoreType.DMA((half_depth,)),
        ],
        compiler_params=pltpu.CompilerParams(
            collective_id=0, has_side_effects=True, vmem_limit_bytes=63 * 2**20
        ),
    )(
        volume,
        w_encode,
        w_down,
        w_bottom,
        w_up,
        w_decode,
        b_encode.reshape(1, -1),
        b_down.reshape(1, -1),
        b_bottom.reshape(1, -1),
        b_up.reshape(1, -1),
        b_decode.reshape(1, -1),
    )


def solution(mesh):
    sizes = (mesh.shape["wide"], mesh.shape["narrow"], mesh.shape["pair"])
    placed = P(("groups", "wide"), "narrow", "pair", None)
    return jax.shard_map(
        functools.partial(body, sizes),
        mesh=mesh,
        in_specs=(placed,) + (P(),) * 10,
        out_specs=placed,
        check_vma=False,
    )
```

time: 99.3 us -> 31.7 us (0.32); the launches traced: 97.7 us -> 31.6 us
  starting transfers between devices: 48.6 us -> 0 us
  Pallas kernels: 0 us -> 29.8 us
  local copies, waits for them, and re-layouts: 18.3 us -> 1.78 us
  matrix products: 13.7 us -> 0 us
  waiting for transfers between devices: 10.7 us -> 0 us
  other arithmetic: 5.5 us -> 0 us
    ppermute x18 -> x0, starting transfers between devices: 48.6 us -> none  [the longest x9 37 us: padded_2(): lax.ppermute(lax.slice_in_dim(block, block.shape[dim] - width, None, axis...]
    pallas_call x0 -> x1, Pallas kernels: none -> 29.8 us  [body(): pl.pallas_call(functools.partial(kernel, sizes), out_shape=jax.ShapeDtype...]
    dot_general x10 -> x0, matrix products: 13.7 us -> none  [the longest x8 11.1 us: conv_taps(): jnp.dot(window_rows.reshape(-1, 9 * channels), weight[offset_a].reshape(9...]
    ppermute x18 -> x0, waiting for transfers between devices: 10.7 us -> none  [the longest x9 5.35 us: padded_2(): lax.ppermute(lax.slice_in_dim(block, block.shape[dim] - width, None, axis...]
    slice x6 -> x0, local copies, waits for them, and re-layouts: 7.11 us -> none  [the longest x3 6.15 us: conv_taps(): weight[offset_a].reshape(9 * channels, outputs)]
    unnamed x59 -> x1, local copies, waits for them, and re-layouts: 8.53 us -> 1.78 us
    concatenate x8 -> x0, other arithmetic: 3.95 us -> none  [padded_2(): block = jnp.concatenate([low, block, high], axis=dim)]
    unnamed x5 -> x0, other arithmetic: 1.48 us -> none
  transfers between devices with their start and end apart: 18 -> 0, of which waited for: 9 -> 0; matrix products, arithmetic and copies ran while one was open for 10% -> 0% of each run, Pallas kernels for 0% -> 0%
where the time goes in v1:
time: 31.7 us; the launch traced here: 31.6 us
  Pallas kernels  29.8 us (94%)
  local copies, waits for them, and re-layouts  1.78 us (6%)
    pallas_call x1, Pallas kernels, body(): pl.pallas_call(functools.partial(kernel, sizes), out_shape=jax.ShapeDtype...  29.8 us
    unnamed x1, local copies, waits for them, and re-layouts  1.78 us

profile of v1, /device:TPU:0, one launch (start us, length us, event | category | flops | bytes accessed | tf_op | source)
XLA Modules:
  0.0 31.6 jit_solution(13561460933777467020)
XLA Ops:
  0.0 29.8 %shard_map.109 = bf16[6,8,32,128]{3,2,1,0:T(8,128)(2,1)} custom-call(bf16[6,8,32,128]{3,2,1,0:T(8,128)(2,1)} %volume.1, bf16[3,3,3,128,128]{4,3,2,1,0:T(8,128)(2,1)} %w_encode.1, bf16[2,2,2,128,256]{4,3,2,1,0:T(8,128)(2,1)} %w_down.1, bf16[3,3,3,256,256]{4,3,2,1,0:T(8,128)(2,1)} %w_bottom.1, bf16[2,2,2,256,128]{4,3,2,1,0:T(8,128)(2,1)} %w_up.1, ...), custom_call_target="tpu_custom_call" | custom-call | tf_op jit(solution)/shard_map/pallas_call | solution.py:500
  29.8 1.8 %copy.13 = bf16[6,8,32,128]{3,2,1,0:T(8,128)(2,1)} copy(bf16[6,8,32,128]{3,2,1,0:T(8,128)(2,1)} %shard_map.109) | data formatting | bytes 786432

commit v2 on v1

v2 whole, which is shorter than its diff:
```python
import functools
import itertools

import jax
import jax.numpy as jnp
from jax import lax
from jax.experimental import pallas as pl
from jax.experimental.pallas import tpu as pltpu
from jax.sharding import PartitionSpec as P

leak_slope = 0.01
MESH = pl.DeviceIdType.MESH
lead = 8
corners = list(itertools.product((0, 1), repeat=2))
plane_steps = [s for s in itertools.product((-1, 0, 1), repeat=2) if s != (0, 0)]
width_steps = (-1, 1)


def leaky_relu(values):
    return jnp.maximum(values, leak_slope * values)


def rounded(values):
    return values.astype(jnp.bfloat16)


def whole_tiles(cells):
    return cells + -cells % 16


def source_span(step, cells, base):
    if step == 0:
        return pl.ds(base, cells)
    return pl.ds(base + (0 if step < 0 else cells - 1), 1)


def target_span(step, cells):
    if step == 0:
        return pl.ds(1, cells)
    return pl.ds(cells + 1 if step < 0 else 0, 1)


def kernel(
    sizes,
    volume,
    w_encode,
    w_down,
    w_bottom,
    w_up,
    w_decode,
    b_encode_far,
    b_down_far,
    b_bottom_far,
    b_up_far,
    b_decode_far,
    decoded,
    v_cells,
    e_cells,
    r_cells,
    c_cells,
    v_frame,
    e_frame,
    r_frame,
    c_frame,
    v_taps,
    e_taps,
    r_taps,
    c_taps,
    edge_out,
    edge_in,
    line_out,
    line_in,
    corner_in,
    c_edge_out,
    c_edge_in,
    c_line_out,
    c_line_in,
    c_corner_in,
    encode_pairs,
    skip_pairs,
    raised_pairs,
    down_matrix,
    bottom_matrix,
    up_matrix,
    down_rows,
    partial,
    result,
    b_encode,
    b_down,
    b_bottom,
    b_up,
    b_decode,
    send_sem,
    recv_sem,
    edge_send_sem,
    edge_recv_sem,
    load_sem,
    store_sem,
):
    depth, height, width, skip = volume.shape
    half_depth, half_height, half_width = depth // 2, height // 2, width // 2
    deep = w_down.shape[-1]
    deep_size, high_size, wide_size = sizes
    at_deep, at_high, at_wide = (lax.axis_index(name) for name in ("wide", "narrow", "pair"))

    def inside(place, step, size):
        return jnp.logical_and(place + step >= 0, place + step < size)

    def exists(step):
        return jnp.logical_and(
            jnp.logical_and(
                inside(at_deep, step[0], deep_size), inside(at_high, step[1], high_size)
            ),
            inside(at_wide, step[2], wide_size),
        )

    def place(step):
        return {"wide": at_deep + step[0], "narrow": at_high + step[1], "pair": at_wide + step[2]}

    plane_used = [
        s
        for s in plane_steps
        if (s[0] == 0 or deep_size > 1) and (s[1] == 0 or high_size > 1)
    ]
    width_used = width_steps if wide_size > 1 else ()
    all_used = [s + (0,) for s in plane_used]
    all_used += [s + (x,) for s in [(0, 0)] + plane_used for x in width_used]

    loads = []

    def load(source, target):
        copy = pltpu.make_async_copy(source, target, load_sem.at[len(loads)])
        copy.start()
        loads.append(copy)
        return copy

    own_load = load(volume, v_cells.at[pl.ds(1, depth), pl.ds(1, height)])

    def load_pairs(weight, first, target):
        return [
            load(
                weight.at[a, :, :, pl.ds(first, skip), :],
                target.at[a, pl.ds(j, 3), :, :, pl.ds(j * skip, skip)],
            )
            for a in range(3)
            for j in range(2)
        ]

    encode_loads = load_pairs(w_encode, 0, encode_pairs)
    encode_loads += [
        load(b_encode_far, b_encode),
        load(b_down_far, b_down),
        load(b_bottom_far, b_bottom),
        load(b_up_far, b_up),
        load(b_decode_far, b_decode),
    ]
    down_load = load(w_down, down_matrix)

    def zero_halo(cells, planes, rows):
        blank = jnp.zeros(cells.shape[2:], cells.dtype)
        for z in range(planes + 2):
            for y in range(rows + 2):
                if z in (0, planes + 1) or y in (0, rows + 1):
                    cells[z, y] = blank

    for cells in (v_cells, e_cells, r_cells):
        zero_halo(cells, depth, height)
    zero_halo(c_cells, half_depth, half_height)
    for arriving in (edge_in, line_in, corner_in, c_edge_in, c_line_in, c_corner_in):
        arriving[...] = jnp.zeros_like(arriving)

    barrier = pltpu.get_barrier_semaphore()
    for step in all_used:

        @pl.when(exists(step))
        def _():
            pl.semaphore_signal(barrier, inc=1, device_id=place(step), device_id_type=MESH)

    pl.semaphore_wait(barrier, sum(exists(step).astype(jnp.int32) for step in all_used))

    started = []

    def send(step, source, target, sends, receives):
        copy = pltpu.make_async_remote_copy(
            src_ref=source,
            dst_ref=target,
            send_sem=sends,
            recv_sem=receives,
            device_id=place(step),
            device_id_type=MESH,
        )
        pl.when(exists(step))(copy.start)
        started.append((exists(step), copy))
        return exists(tuple(-offset for offset in step)), copy

    def send_planes(slot, cells, source, base, planes, rows):
        return [
            send(
                step + (0,),
                source.at[source_span(step[0], planes, base), source_span(step[1], rows, base)],
                cells.at[target_span(step[0], planes), target_span(step[1], rows)],
                send_sem.at[slot, k],
                recv_sem.at[slot, k],
            )
            for k, step in enumerate(plane_used)
        ]

    def send_edges(slot, edges, lines, arriving, arriving_lines, arriving_corners, planes, rows):
        slab = whole_tiles(rows + 2)
        copies = []
        for n, step in enumerate([(0, 0)] + plane_used):
            for k, across in enumerate(width_used):
                if step[0] == 0:
                    here = there = pl.ds(slab, planes * slab)
                else:
                    here = pl.ds((1 if step[0] < 0 else planes) * slab, slab)
                    there = pl.ds((planes + 1 if step[0] < 0 else 0) * slab, slab)
                side = 1 if step[1] < 0 else 0
                if step[1] == 0:
                    source, target = edges.at[k, here], arriving.at[k, there]
                elif step[0] == 0:
                    source, target = lines.at[k, 1 - side], arriving_lines.at[k, side]
                else:
                    corner = corners.index((1 if step[0] < 0 else 0, side))
                    source, target = edges.at[k, here], arriving_corners.at[k, corner]
                copies.append(
                    send(
                        step + (across,),
                        source,
                        target,
                        edge_send_sem.at[slot, k, n],
                        edge_recv_sem.at[slot, k, n],
                    )
                )
        return copies

    def arrive(copies):
        for coming, copy in copies:
            pl.when(coming)(copy.wait_recv)

    def take_edges(frame, edges, lines, planes, rows, cells):
        slab = whole_tiles(rows + 2)
        count, pitch, channels = frame.shape
        flat = frame.reshape(count * pitch, channels)
        for k, column in enumerate((lead, lead + cells - 1)):
            edges[k] = rounded(flat[pl.ds(column, (planes + 2) * slab, stride=pitch), :])
            for j, y in enumerate((1, rows)):
                lines[k, j] = rounded(
                    flat[pl.ds(y * pitch + column, count // slab, stride=slab * pitch), :]
                )

    def put_edges(frame, arriving, arriving_lines, arriving_corners, planes, rows, cells):
        slab = whole_tiles(rows + 2)
        count, pitch, channels = frame.shape
        flat = frame.reshape(count * pitch, channels)
        for k, column in enumerate((lead + cells, lead - 1)):
            flat[pl.ds(column, (planes + 2) * slab, stride=pitch), :] = arriving[k].astype(
                jnp.float32
            )
            for j, y in enumerate((0, rows + 1)):
                flat[
                    pl.ds(y * pitch + column, count // slab, stride=slab * pitch), :
                ] = arriving_lines[k, j].astype(jnp.float32)
            for n, (deep_side, high_side) in enumerate(corners):
                plane = deep_side * (planes + 1) * slab + high_side * (rows + 1)
                row = 1 if high_side else rows
                frame[plane, column : column + 1, :] = arriving_corners[k, n].astype(jnp.float32)[
                    row : row + 1
                ]

    def lanes(h):
        return pl.ds(h * skip, skip)

    def halo_to_frame(cells, frame, planes, rows, span):
        for z in range(planes + 2):
            for y in range(rows + 2):
                if z in (0, planes + 1) or y in (0, rows + 1):
                    frame[z * whole_tiles(rows + 2) + y, lead : lead + span, :] = cells[z, y].astype(
                        jnp.float32
                    )

    deep_parts = range(deep // skip)

    slab = whole_tiles(height + 2)
    low_slab = whole_tiles(half_height + 2)
    middle = width // 2

    def spread(frame, taps, z, y, c, first, cells):
        begin = lead - 1 + c + first
        taps[z, y // 2, y % 2, first : first + cells, c * skip : (c + 1) * skip] = rounded(
            frame[z * slab + y, begin : begin + cells, :]
        )

    def spread_own(frame, taps):
        def one(z, carry):
            for y in range(1, height + 1):
                spread(frame, taps, z, y, 0, middle, middle)
                spread(frame, taps, z, y, 1, 0, width)
                spread(frame, taps, z, y, 2, 0, middle)
            return carry

        lax.fori_loop(1, depth + 1, one, 0)

    def spread_rest(frame, taps):
        def one(z, carry):
            for y in range(1, height + 1):
                spread(frame, taps, z, y, 0, 0, middle)
                spread(frame, taps, z, y, 2, middle, middle)
            for y, c in itertools.product((0, height + 1), range(3)):
                spread(frame, taps, z, y, c, 0, width)
            return carry

        lax.fori_loop(1, depth + 1, one, 0)
        for z in (0, depth + 1):
            for y, c in itertools.product(range(height + 2), range(3)):
                spread(frame, taps, z, y, c, 0, width)

    def pair_conv(taps, matrix, z):
        total = None
        for a in range(3):
            rows = jnp.concatenate(
                [
                    taps[pl.ds(z + a, 2), pl.ds(r // 2, half_height), r % 2].reshape(
                        2 * half_height * width, 3 * skip
                    )
                    for r in range(4)
                ],
                axis=-1,
            )
            term = jnp.dot(
                rows,
                matrix[a].reshape(12 * skip, 2 * skip),
                preferred_element_type=jnp.float32,
            )
            total = term if total is None else total + term
        return total

    v_copies = send_planes(0, v_cells, volume, 0, depth, height)
    own_load.wait()

    def widen(z, carry):
        for y in range(1, height + 1):
            v_frame[z * slab + y, lead : lead + width, :] = v_cells[z, y].astype(jnp.float32)
        return carry

    lax.fori_loop(1, depth + 1, widen, 0)

    def begin_edges(slot, frame, n):
        take_edges(frame, edge_out.at[n], line_out.at[n], depth, height, width)
        arriving = (edge_in.at[n], line_in.at[n], corner_in.at[n])
        copies = send_edges(
            slot, edge_out.at[n], line_out.at[n], *arriving, depth, height
        )
        return arriving, copies

    v_arriving, v_edges = begin_edges(0, v_frame, 0)
    bottom_load = load(w_bottom, bottom_matrix)
    skip_loads = load_pairs(w_decode, skip, skip_pairs)
    up_loads = [
        load(
            w_up.at[a, b, c],
            up_matrix.at[:, pl.ds(((a * 2 + b) * 2 + c) * skip, skip)],
        )
        for a, b, c in itertools.product((0, 1), repeat=3)
    ]
    raised_loads = load_pairs(w_decode, 0, raised_pairs)
    for pairs in (encode_pairs, skip_pairs, raised_pairs):
        for a in range(3):
            pairs[a, 0, :, :, skip : 2 * skip] = jnp.zeros((3, skip, skip), jnp.bfloat16)
            pairs[a, 3, :, :, 0:skip] = jnp.zeros((3, skip, skip), jnp.bfloat16)
    spread_own(v_frame, v_taps)
    arrive(v_copies)
    halo_to_frame(v_cells, v_frame, depth, height, width)
    arrive(v_edges)
    put_edges(v_frame, *v_arriving, depth, height, width)
    spread_rest(v_frame, v_taps)
    for copy in encode_loads:
        copy.wait()
    encode_bias = jnp.concatenate([b_encode[...], b_encode[...]], axis=-1)

    def encode(i, carry):
        z = 2 * i
        values = rounded(leaky_relu(pair_conv(v_taps, encode_pairs, z) + encode_bias))
        values = values.reshape(2, half_height, width, 2 * skip)
        for dz in range(2):
            for y in range(height):
                cells = values[dz, y // 2, :, (y % 2) * skip : (y % 2 + 1) * skip]
                e_cells[z + dz + 1, y + 1] = cells
                e_frame[(z + dz + 1) * slab + y + 1, lead : lead + width, :] = cells.astype(
                    jnp.float32
                )
        return carry

    lax.fori_loop(0, half_depth, encode, 0)

    def gather_down(z, carry):
        for y in range(half_height):
            for a, b, c in itertools.product((0, 1), repeat=3):
                tap = (a * 2 + b) * 2 + c
                down_rows[z, y, :, tap * skip : (tap + 1) * skip] = rounded(
                    e_frame[
                        (2 * z + a + 1) * slab + 2 * y + b + 1,
                        pl.ds(lead + c, half_width, stride=2),
                        :,
                    ]
                )
        return carry

    lax.fori_loop(0, half_depth, gather_down, 0)
    down_load.wait()
    low_cells = half_depth * half_height * half_width
    coarse = jnp.dot(
        down_rows[...].reshape(low_cells, 8 * skip),
        down_matrix[...].reshape(8 * skip, deep),
        preferred_element_type=jnp.float32,
    )
    coarse = rounded(leaky_relu(coarse + b_down[...]))
    coarse = coarse.reshape(half_depth, half_height, half_width, deep)
    c_cells[1 : 1 + half_depth, 1 : 1 + half_height] = coarse
    c_copies = send_planes(2, c_cells, c_cells, 1, half_depth, half_height)
    for z in range(half_depth):
        for y in range(half_height):
            for h in deep_parts:
                c_frame[
                    h, (z + 1) * low_slab + y + 1, lead : lead + half_width, :
                ] = coarse[z, y, :, h * skip : (h + 1) * skip].astype(jnp.float32)

    low = (half_depth, half_height, half_width)
    c_edges = []
    for h in deep_parts:
        take_edges(
            c_frame.at[h], c_edge_out.at[:, :, lanes(h)], c_line_out.at[:, :, :, lanes(h)], *low
        )
    c_edges = send_edges(
        2, c_edge_out, c_line_out, c_edge_in, c_line_in, c_corner_in, half_depth, half_height
    )
    e_copies = send_planes(1, e_cells, e_cells, 1, depth, height)
    e_arriving, e_edges = begin_edges(1, e_frame, 1)
    spread_own(e_frame, e_taps)

    def decode_skip(i):
        partial[i] = pair_conv(e_taps, skip_pairs, 2 * i)

    arrive(c_copies)
    for h in deep_parts:
        halo_to_frame(c_cells.at[:, :, :, lanes(h)], c_frame.at[h], *low)
    arrive(c_edges)
    for h in deep_parts:
        put_edges(
            c_frame.at[h],
            c_edge_in.at[:, :, lanes(h)],
            c_line_in.at[:, :, :, lanes(h)],
            c_corner_in.at[:, :, :, lanes(h)],
            *low,
        )
    for z in range(half_depth + 2):
        for y in range(half_height + 2):
            for c, h in itertools.product(range(3), deep_parts):
                first = c * deep + h * skip
                c_taps[z, y, :, first : first + skip] = rounded(
                    c_frame[
                        h, z * low_slab + y, lead - 1 + c : lead - 1 + c + half_width, :
                    ]
                )
    bottom_load.wait()
    total = jnp.zeros((low_cells, deep), jnp.float32)
    for a in range(3):
        for b in range(3):
            total += jnp.dot(
                c_taps[a : a + half_depth, b : b + half_height].reshape(low_cells, 3 * deep),
                bottom_matrix[a, b].reshape(3 * deep, deep),
                preferred_element_type=jnp.float32,
            )
    bottom = rounded(leaky_relu(total + b_bottom[...]))
    for copy in up_loads:
        copy.wait()
    up_bias = jnp.concatenate([b_up[...], b_up[...]], axis=-1)
    for a in range(2):
        for b in range(2):
            first = (a * 2 + b) * 2 * skip
            lifted = jnp.dot(
                bottom, up_matrix[:, first : first + 2 * skip], preferred_element_type=jnp.float32
            )
            lifted = rounded(lifted + up_bias).astype(jnp.float32)
            lifted = lifted.reshape(half_depth, half_height, half_width, 2 * skip)
            for z in range(half_depth):
                for y in range(half_height):
                    plane = (2 * z + a + 1) * slab + 2 * y + b + 1
                    for c in range(2):
                        r_frame[plane, pl.ds(lead + c, half_width, stride=2), :] = lifted[
                            z, y, :, c * skip : (c + 1) * skip
                        ]

    def narrow_raised(z, carry):
        for y in range(height):
            r_cells[z + 1, y + 1] = rounded(
                r_frame[(z + 1) * slab + y + 1, lead : lead + width, :]
            )
        return carry

    lax.fori_loop(0, depth, narrow_raised, 0)
    r_copies = send_planes(3, r_cells, r_cells, 1, depth, height)

    r_arriving, r_edges = begin_edges(3, r_frame, 2)
    spread_own(r_frame, r_taps)
    arrive(e_copies)
    halo_to_frame(e_cells, e_frame, depth, height, width)
    arrive(e_edges)
    put_edges(e_frame, *e_arriving, depth, height, width)
    spread_rest(e_frame, e_taps)
    for copy in skip_loads:
        copy.wait()
    for i in range(half_depth):
        decode_skip(i)
    arrive(r_copies)
    halo_to_frame(r_cells, r_frame, depth, height, width)
    arrive(r_edges)
    put_edges(r_frame, *r_arriving, depth, height, width)
    spread_rest(r_frame, r_taps)
    for copy in raised_loads:
        copy.wait()
    decode_bias = jnp.concatenate([b_decode[...], b_decode[...]], axis=-1)
    stores = []
    for i in range(half_depth):
        values = pair_conv(r_taps, raised_pairs, 2 * i) + partial[i]
        values = (values + decode_bias).reshape(2, half_height, width, 2 * skip)
        for dz in range(2):
            for y in range(height):
                result[2 * i + dz, y] = values[
                    dz, y // 2, :, (y % 2) * skip : (y % 2 + 1) * skip
                ]
        store = pltpu.make_async_copy(
            result.at[pl.ds(2 * i, 2)], decoded.at[pl.ds(2 * i, 2)], store_sem.at[i]
        )
        store.start()
        stores.append(store)
    for going, copy in started:
        pl.when(going)(copy.wait_send)
    for store in stores:
        store.wait()


def body(
    sizes,
    volume,
    w_encode,
    b_encode,
    w_down,
    b_down,
    w_bottom,
    b_bottom,
    w_up,
    b_up,
    w_decode,
    b_decode,
):
    depth, height, width, skip = volume.shape
    deep = w_down.shape[-1]
    half_depth, half_height, half_width = depth // 2, height // 2, width // 2
    planes, low_planes = depth + 2, half_depth + 2
    slab, low_slab = whole_tiles(height + 2), whole_tiles(half_height + 2)
    line, low_line = whole_tiles(planes), whole_tiles(low_planes)
    half = jnp.bfloat16
    cells = pltpu.VMEM((depth + 2, height + 2, width, skip), half)
    frame = pltpu.VMEM((line * slab, width + 2 * lead, skip), jnp.float32)
    taps = pltpu.VMEM((depth + 2, height // 2 + 1, 2, width, 3 * skip), half)
    pairs = pltpu.VMEM((3, 4, 3, skip, 2 * skip), half)
    far = pl.BlockSpec(memory_space=pltpu.HBM)
    bias = lambda size: pltpu.VMEM((1, size), jnp.float32)
    total = pl.pallas_call(
        functools.partial(kernel, sizes),
        out_shape=jax.ShapeDtypeStruct(volume.shape, jnp.float32),
        in_specs=[far] * 11,
        out_specs=far,
        scratch_shapes=[
            cells,
            cells,
            cells,
            pltpu.VMEM((half_depth + 2, half_height + 2, half_width, deep), half),
            frame,
            frame,
            frame,
            pltpu.VMEM((deep // skip, low_line * low_slab, half_width + 2 * lead, skip), jnp.float32),
            taps,
            taps,
            taps,
            pltpu.VMEM((half_depth + 2, half_height + 2, half_width, 3 * deep), half),
            pltpu.VMEM((3, 2, planes * slab, skip), half),
            pltpu.VMEM((3, 2, planes * slab, skip), half),
            pltpu.VMEM((3, 2, 2, line, skip), half),
            pltpu.VMEM((3, 2, 2, line, skip), half),
            pltpu.VMEM((3, 2, 4, slab, skip), half),
            pltpu.VMEM((2, low_planes * low_slab, deep), half),
            pltpu.VMEM((2, low_planes * low_slab, deep), half),
            pltpu.VMEM((2, 2, low_line, deep), half),
            pltpu.VMEM((2, 2, low_line, deep), half),
            pltpu.VMEM((2, 4, low_slab, deep), half),
            pairs,
            pairs,
            pairs,
            pltpu.VMEM(w_down.shape, half),
            pltpu.VMEM(w_bottom.shape, half),
            pltpu.VMEM((deep, 8 * skip), half),
            pltpu.VMEM((half_depth, half_height, half_width, 8 * skip), half),
            pltpu.VMEM((half_depth, height * width, 2 * skip), jnp.float32),
            pltpu.VMEM(volume.shape, jnp.float32),
            bias(skip),
            bias(deep),
            bias(deep),
            bias(skip),
            bias(skip),
            pltpu.SemaphoreType.DMA((4, 8)),
            pltpu.SemaphoreType.DMA((4, 8)),
            pltpu.SemaphoreType.DMA((4, 2, 9)),
            pltpu.SemaphoreType.DMA((4, 2, 9)),
            pltpu.SemaphoreType.DMA((34,)),
            pltpu.SemaphoreType.DMA((half_depth,)),
        ],
        compiler_params=pltpu.CompilerParams(
            collective_id=0, has_side_effects=True, vmem_limit_bytes=63 * 2**20
        ),
    )(
        volume,
        w_encode,
        w_down,
        w_bottom,
        w_up,
        w_decode,
        b_encode.reshape(1, -1),
        b_down.reshape(1, -1),
        b_bottom.reshape(1, -1),
        b_up.reshape(1, -1),
        b_decode.reshape(1, -1),
    )
    return rounded(leaky_relu(total))


def solution(mesh):
    sizes = (mesh.shape["wide"], mesh.shape["narrow"], mesh.shape["pair"])
    placed = P(("groups", "wide"), "narrow", "pair", None)
    return jax.shard_map(
        functools.partial(body, sizes),
        mesh=mesh,
        in_specs=(placed,) + (P(),) * 10,
        out_specs=placed,
        check_vma=False,
    )
```

time: 31.7 us -> 30.2 us (0.953)
  other arithmetic: 0 us -> 1.98 us
  local copies, waits for them, and re-layouts: 1.78 us -> 0 us
  Pallas kernels: 29.8 us -> 28.1 us
    convert_element_type x0 -> x1, other arithmetic: none -> 1.98 us  [rounded(): return values.astype(jnp.bfloat16)]
    unnamed x1 -> x0, local copies, waits for them, and re-layouts: 1.78 us -> none
    pallas_call x1, Pallas kernels: 29.8 us -> 28.1 us  [body(): pl.pallas_call(functools.partial(kernel, sizes), out_shape=jax.ShapeDtype...]
where the time goes in v2:
time: 30.2 us; the launch traced here: 30.1 us
  Pallas kernels  28.1 us (93%)
  other arithmetic  1.98 us (7%)
    pallas_call x1, Pallas kernels, body(): pl.pallas_call(functools.partial(kernel, sizes), out_shape=jax.ShapeDtype...  28.1 us
    convert_element_type x1, other arithmetic, rounded(): return values.astype(jnp.bfloat16)  1.98 us

profile of v2, /device:TPU:0, one launch (start us, length us, event | category | flops | bytes accessed | tf_op | source)
XLA Modules:
  0.0 30.1 jit_solution(15552974878635449073)
XLA Ops:
  0.0 28.1 %shard_map.109 = f32[6,8,32,128]{3,2,1,0:T(8,128)} custom-call(bf16[6,8,32,128]{3,2,1,0:T(8,128)(2,1)} %volume.1, bf16[3,3,3,128,128]{4,3,2,1,0:T(8,128)(2,1)} %w_encode.1, bf16[2,2,2,128,256]{4,3,2,1,0:T(8,128)(2,1)} %w_down.1, bf16[3,3,3,256,256]{4,3,2,1,0:T(8,128)(2,1)} %w_bottom.1, bf16[2,2,2,256,128]{4,3,2,1,0:T(8,128)(2,1)} %w_up.1, ...), custom_call_target="tpu_custom_call" | custom-call | tf_op jit(solution)/shard_map/pallas_call | solution.py:570
  28.1 2.0 %fusion = bf16[6,8,32,128]{3,2,1,0:T(8,128)(2,1)} fusion(f32[6,8,32,128]{3,2,1,0:T(8,128)} %shard_map.109), kind=kLoop, calls=%fused_computation.1 | loop fusion | flops 589824 | bytes 1179648 | tf_op jit(solution)/shard_map/convert_element_type | solution.py:24

commit v3 on v2

--- a/solution.py
+++ b/solution.py
@@ -315,13 +315,12 @@
             for y, c in itertools.product(range(height + 2), range(3)):
                 spread(frame, taps, z, y, c, 0, width)
 
-    def pair_conv(taps, matrix, z):
-        total = None
+    def pair_conv(taps, matrix, fresh):
         for a in range(3):
             rows = jnp.concatenate(
                 [
-                    taps[pl.ds(z + a, 2), pl.ds(r // 2, half_height), r % 2].reshape(
-                        2 * half_height * width, 3 * skip
+                    taps[a : a + depth, r // 2 : r // 2 + half_height, r % 2].reshape(
+                        depth * half_height * width, 3 * skip
                     )
                     for r in range(4)
                 ],
@@ -332,8 +331,10 @@
                 matrix[a].reshape(12 * skip, 2 * skip),
                 preferred_element_type=jnp.float32,
             )
-            total = term if total is None else total + term
-        return total
+            if a == 0 and fresh:
+                partial[...] = term
+            else:
+                partial[...] += term
 
     v_copies = send_planes(0, v_cells, volume, 0, depth, height)
     own_load.wait()
@@ -378,20 +379,20 @@
         copy.wait()
     encode_bias = jnp.concatenate([b_encode[...], b_encode[...]], axis=-1)
 
-    def encode(i, carry):
-        z = 2 * i
-        values = rounded(leaky_relu(pair_conv(v_taps, encode_pairs, z) + encode_bias))
-        values = values.reshape(2, half_height, width, 2 * skip)
-        for dz in range(2):
-            for y in range(height):
-                cells = values[dz, y // 2, :, (y % 2) * skip : (y % 2 + 1) * skip]
-                e_cells[z + dz + 1, y + 1] = cells
-                e_frame[(z + dz + 1) * slab + y + 1, lead : lead + width, :] = cells.astype(
-                    jnp.float32
-                )
+    pair_conv(v_taps, encode_pairs, True)
+    sheet = half_height * width
+
+    def encode(z, carry):
+        values = partial[pl.ds(pl.multiple_of(z * sheet, sheet), sheet), :]
+        values = rounded(leaky_relu(values + encode_bias))
+        values = values.reshape(half_height, width, 2 * skip)
+        for y in range(height):
+            cells = values[y // 2, :, (y % 2) * skip : (y % 2 + 1) * skip]
+            e_cells[z + 1, y + 1] = cells
+            e_frame[(z + 1) * slab + y + 1, lead : lead + width, :] = cells.astype(jnp.float32)
         return carry
 
-    lax.fori_loop(0, half_depth, encode, 0)
+    lax.fori_loop(0, depth, encode, 0)
 
     def gather_down(z, carry):
         for y in range(half_height):
@@ -437,9 +438,6 @@
     e_copies = send_planes(1, e_cells, e_cells, 1, depth, height)
     e_arriving, e_edges = begin_edges(1, e_frame, 1)
     spread_own(e_frame, e_taps)
-
-    def decode_skip(i):
-        partial[i] = pair_conv(e_taps, skip_pairs, 2 * i)
 
     arrive(c_copies)
     for h in deep_parts:
@@ -510,8 +508,7 @@
     spread_rest(e_frame, e_taps)
     for copy in skip_loads:
         copy.wait()
-    for i in range(half_depth):
-        decode_skip(i)
+    pair_conv(e_taps, skip_pairs, True)
     arrive(r_copies)
     halo_to_frame(r_cells, r_frame, depth, height, width)
     arrive(r_edges)
@@ -520,24 +517,21 @@
     for copy in raised_loads:
         copy.wait()
     decode_bias = jnp.concatenate([b_decode[...], b_decode[...]], axis=-1)
-    stores = []
-    for i in range(half_depth):
-        values = pair_conv(r_taps, raised_pairs, 2 * i) + partial[i]
-        values = (values + decode_bias).reshape(2, half_height, width, 2 * skip)
-        for dz in range(2):
-            for y in range(height):
-                result[2 * i + dz, y] = values[
-                    dz, y // 2, :, (y % 2) * skip : (y % 2 + 1) * skip
-                ]
-        store = pltpu.make_async_copy(
-            result.at[pl.ds(2 * i, 2)], decoded.at[pl.ds(2 * i, 2)], store_sem.at[i]
-        )
-        store.start()
-        stores.append(store)
+    pair_conv(r_taps, raised_pairs, False)
+
+    def finish(z, carry):
+        values = partial[pl.ds(pl.multiple_of(z * sheet, sheet), sheet), :]
+        values = (values + decode_bias).reshape(half_height, width, 2 * skip)
+        for y in range(height):
+            result[z, y] = values[y // 2, :, (y % 2) * skip : (y % 2 + 1) * skip]
+        return carry
+
+    lax.fori_loop(0, depth, finish, 0)
+    store = pltpu.make_async_copy(result, decoded, store_sem)
+    store.start()
     for going, copy in started:
         pl.when(going)(copy.wait_send)
-    for store in stores:
-        store.wait()
+    store.wait()
 
 
 def body(
@@ -602,7 +596,7 @@
             pltpu.VMEM(w_bottom.shape, half),
             pltpu.VMEM((deep, 8 * skip), half),
             pltpu.VMEM((half_depth, half_height, half_width, 8 * skip), half),
-            pltpu.VMEM((half_depth, height * width, 2 * skip), jnp.float32),
+            pltpu.VMEM((depth * height * width // 2, 2 * skip), jnp.float32),
             pltpu.VMEM(volume.shape, jnp.float32),
             bias(skip),
             bias(deep),
@@ -614,7 +608,7 @@
             pltpu.SemaphoreType.DMA((4, 2, 9)),
             pltpu.SemaphoreType.DMA((4, 2, 9)),
             pltpu.SemaphoreType.DMA((34,)),
-            pltpu.SemaphoreType.DMA((half_depth,)),
+            pltpu.SemaphoreType.DMA,
         ],
         compiler_params=pltpu.CompilerParams(
             collective_id=0, has_side_effects=True, vmem_limit_bytes=63 * 2**20

time: 30.2 us -> 33.3 us (1.10)
  Pallas kernels: 28.1 us -> 31.2 us
    pallas_call x1, Pallas kernels: 28.1 us -> 31.2 us  [body(): pl.pallas_call(functools.partial(kernel, sizes), out_shape=jax.ShapeDtype...]
where the time goes in v3:
time: 33.3 us; the launch traced here: 33.2 us
  Pallas kernels  31.2 us (94%)
  other arithmetic  1.98 us (6%)
    pallas_call x1, Pallas kernels, body(): pl.pallas_call(functools.partial(kernel, sizes), out_shape=jax.ShapeDtype...  31.2 us
    convert_element_type x1, other arithmetic, rounded(): return values.astype(jnp.bfloat16)  1.98 us

profile of v3, /device:TPU:0, one launch (start us, length us, event | category | flops | bytes accessed | tf_op | source)
XLA Modules:
  0.0 33.2 jit_solution(3238266612365430063)
XLA Ops:
  0.0 31.2 %shard_map.109 = f32[6,8,32,128]{3,2,1,0:T(8,128)} custom-call(bf16[6,8,32,128]{3,2,1,0:T(8,128)(2,1)} %volume.1, bf16[3,3,3,128,128]{4,3,2,1,0:T(8,128)(2,1)} %w_encode.1, bf16[2,2,2,128,256]{4,3,2,1,0:T(8,128)(2,1)} %w_down.1, bf16[3,3,3,256,256]{4,3,2,1,0:T(8,128)(2,1)} %w_bottom.1, bf16[2,2,2,256,128]{4,3,2,1,0:T(8,128)(2,1)} %w_up.1, ...), custom_call_target="tpu_custom_call" | custom-call | tf_op jit(solution)/shard_map/pallas_call | solution.py:564
  31.2 2.0 %fusion = bf16[6,8,32,128]{3,2,1,0:T(8,128)(2,1)} fusion(f32[6,8,32,128]{3,2,1,0:T(8,128)} %shard_map.109), kind=kLoop, calls=%fused_computation.1 | loop fusion | flops 589824 | bytes 1179648 | tf_op jit(solution)/shard_map/convert_element_type | solution.py:24

commit v4 on v2

--- a/solution.py
+++ b/solution.py
@@ -84,7 +84,6 @@
     up_matrix,
     down_rows,
     partial,
-    result,
     b_encode,
     b_down,
     b_bottom,
@@ -95,7 +94,6 @@
     edge_send_sem,
     edge_recv_sem,
     load_sem,
-    store_sem,
 ):
     depth, height, width, skip = volume.shape
     half_depth, half_height, half_width = depth // 2, height // 2, width // 2
@@ -107,24 +105,31 @@
         return jnp.logical_and(place + step >= 0, place + step < size)
 
     def exists(step):
-        return jnp.logical_and(
-            jnp.logical_and(
-                inside(at_deep, step[0], deep_size), inside(at_high, step[1], high_size)
-            ),
-            inside(at_wide, step[2], wide_size),
+        near = jnp.logical_and(
+            inside(at_deep, step[0], deep_size), inside(at_high, step[1], high_size)
         )
+        if step[2] is None:
+            return near
+        return jnp.logical_and(near, inside(at_wide, step[2], wide_size))
+
+    def reverse(step):
+        return tuple(None if offset is None else -offset for offset in step)
 
     def place(step):
-        return {"wide": at_deep + step[0], "narrow": at_high + step[1], "pair": at_wide + step[2]}
+        column = 1 - at_wide if step[2] is None else at_wide + step[2]
+        return {"wide": at_deep + step[0], "narrow": at_high + step[1], "pair": column}
 
     plane_used = [
         s
         for s in plane_steps
         if (s[0] == 0 or deep_size > 1) and (s[1] == 0 or high_size > 1)
     ]
-    width_used = width_steps if wide_size > 1 else ()
+    if wide_size == 2:
+        width_used = ((None, 1 - at_wide),)
+    else:
+        width_used = tuple(zip(width_steps, (0, 1))) if wide_size > 1 else ()
     all_used = [s + (0,) for s in plane_used]
-    all_used += [s + (x,) for s in [(0, 0)] + plane_used for x in width_used]
+    all_used += [s + (x,) for s in [(0, 0)] + plane_used for x, _ in width_used]
 
     loads = []
 
@@ -191,7 +196,7 @@
         )
         pl.when(exists(step))(copy.start)
         started.append((exists(step), copy))
-        return exists(tuple(-offset for offset in step)), copy
+        return exists(reverse(step)), copy
 
     def send_planes(slot, cells, source, base, planes, rows):
         return [
@@ -209,7 +214,7 @@
         slab = whole_tiles(rows + 2)
         copies = []
         for n, step in enumerate([(0, 0)] + plane_used):
-            for k, across in enumerate(width_used):
+            for lane, (across, k) in enumerate(width_used):
                 if step[0] == 0:
                     here = there = pl.ds(slab, planes * slab)
                 else:
@@ -228,8 +233,8 @@
                         step + (across,),
                         source,
                         target,
-                        edge_send_sem.at[slot, k, n],
-                        edge_recv_sem.at[slot, k, n],
+                        edge_send_sem.at[slot, lane, n],
+                        edge_recv_sem.at[slot, lane, n],
                     )
                 )
         return copies
@@ -311,9 +316,13 @@
             return carry
 
         lax.fori_loop(1, depth + 1, one, 0)
-        for z in (0, depth + 1):
+
+        def outer(i, carry):
             for y, c in itertools.product(range(height + 2), range(3)):
-                spread(frame, taps, z, y, c, 0, width)
+                spread(frame, taps, i * (depth + 1), y, c, 0, width)
+            return carry
+
+        lax.fori_loop(0, 2, outer, 0)
 
     def pair_conv(taps, matrix, z):
         total = None
@@ -438,8 +447,9 @@
     e_arriving, e_edges = begin_edges(1, e_frame, 1)
     spread_own(e_frame, e_taps)
 
-    def decode_skip(i):
+    def decode_skip(i, carry):
         partial[i] = pair_conv(e_taps, skip_pairs, 2 * i)
+        return carry
 
     arrive(c_copies)
     for h in deep_parts:
@@ -510,8 +520,7 @@
     spread_rest(e_frame, e_taps)
     for copy in skip_loads:
         copy.wait()
-    for i in range(half_depth):
-        decode_skip(i)
+    lax.fori_loop(0, half_depth, decode_skip, 0)
     arrive(r_copies)
     halo_to_frame(r_cells, r_frame, depth, height, width)
     arrive(r_edges)
@@ -520,24 +529,18 @@
     for copy in raised_loads:
         copy.wait()
     decode_bias = jnp.concatenate([b_decode[...], b_decode[...]], axis=-1)
-    stores = []
-    for i in range(half_depth):
+
+    def decode(i, carry):
         values = pair_conv(r_taps, raised_pairs, 2 * i) + partial[i]
         values = (values + decode_bias).reshape(2, half_height, width, 2 * skip)
         for dz in range(2):
             for y in range(height):
-                result[2 * i + dz, y] = values[
-                    dz, y // 2, :, (y % 2) * skip : (y % 2 + 1) * skip
-                ]
-        store = pltpu.make_async_copy(
-            result.at[pl.ds(2 * i, 2)], decoded.at[pl.ds(2 * i, 2)], store_sem.at[i]
-        )
-        store.start()
-        stores.append(store)
+                decoded[2 * i + dz, y] = values[dz, y // 2, :, (y % 2) * skip : (y % 2 + 1) * skip]
+        return carry
+
+    lax.fori_loop(0, half_depth, decode, 0)
     for going, copy in started:
         pl.when(going)(copy.wait_send)
-    for store in stores:
-        store.wait()
 
 
 def body(
@@ -567,11 +570,13 @@
     pairs = pltpu.VMEM((3, 4, 3, skip, 2 * skip), half)
     far = pl.BlockSpec(memory_space=pltpu.HBM)
     bias = lambda size: pltpu.VMEM((1, size), jnp.float32)
+    operands = (volume, w_encode, w_down, w_bottom, w_up, w_decode)
+    operands += tuple(b.reshape(1, -1) for b in (b_encode, b_down, b_bottom, b_up, b_decode))
     total = pl.pallas_call(
         functools.partial(kernel, sizes),
         out_shape=jax.ShapeDtypeStruct(volume.shape, jnp.float32),
         in_specs=[far] * 11,
-        out_specs=far,
+        out_specs=pl.BlockSpec(memory_space=pltpu.VMEM),
         scratch_shapes=[
             cells,
             cells,
@@ -603,7 +608,6 @@
             pltpu.VMEM((deep, 8 * skip), half),
             pltpu.VMEM((half_depth, half_height, half_width, 8 * skip), half),
             pltpu.VMEM((half_depth, height * width, 2 * skip), jnp.float32),
-            pltpu.VMEM(volume.shape, jnp.float32),
             bias(skip),
             bias(deep),
             bias(deep),
@@ -614,23 +618,12 @@
             pltpu.SemaphoreType.DMA((4, 2, 9)),
             pltpu.SemaphoreType.DMA((4, 2, 9)),
             pltpu.SemaphoreType.DMA((34,)),
-            pltpu.SemaphoreType.DMA((half_depth,)),
         ],
         compiler_params=pltpu.CompilerParams(
-            collective_id=0, has_side_effects=True, vmem_limit_bytes=63 * 2**20
+            collective_id=0, has_side_effects=True, vmem_limit_bytes=52 * 2**20
         ),
     )(
-        volume,
-        w_encode,
-        w_down,
-        w_bottom,
-        w_up,
-        w_decode,
-        b_encode.reshape(1, -1),
-        b_down.reshape(1, -1),
-        b_bottom.reshape(1, -1),
-        b_up.reshape(1, -1),
-        b_decode.reshape(1, -1),
+        *(pltpu.with_memory_space_constraint(x, pltpu.HBM) for x in operands)
     )
     return rounded(leaky_relu(total))
 

time: 30.2 us -> 27.8 us (0.921)
  Pallas kernels: 28.1 us -> 26.8 us
  other arithmetic: 1.98 us -> 0.84 us
    pallas_call x1, Pallas kernels: 28.1 us -> 26.8 us  [body(): pl.pallas_call(functools.partial(kernel, sizes), out_shape=jax.ShapeDtype...]
    convert_element_type x1, other arithmetic: 1.98 us -> 0.84 us  [rounded(): return values.astype(jnp.bfloat16)]
where the time goes in v4:
time: 27.8 us; the launch traced here: 27.6 us
  Pallas kernels  26.8 us (96%)
  other arithmetic  0.84 us (3%)
    pallas_call x1, Pallas kernels, body(): pl.pallas_call(functools.partial(kernel, sizes), out_shape=jax.ShapeDtype...  26.8 us
    convert_element_type x1, other arithmetic, rounded(): return values.astype(jnp.bfloat16)  0.84 us

profile of v4, /device:TPU:0, one launch (start us, length us, event | category | flops | bytes accessed | tf_op | source)
XLA Modules:
  0.0 27.6 jit_solution(13861894781118801354)
XLA Ops:
  0.0 26.8 %shard_map.109 = f32[6,8,32,128]{3,2,1,0:T(8,128)S(1)} custom-call(bf16[6,8,32,128]{3,2,1,0:T(8,128)(2,1)} %volume.1, bf16[3,3,3,128,128]{4,3,2,1,0:T(8,128)(2,1)} %w_encode.1, bf16[2,2,2,128,256]{4,3,2,1,0:T(8,128)(2,1)} %w_down.1, bf16[3,3,3,256,256]{4,3,2,1,0:T(8,128)(2,1)} %w_bottom.1, bf16[2,2,2,256,128]{4,3,2,1,0:T(8,128)(2,1)} %w_up.1, ...), custom_call_target="tpu_custom_call" | custom-call | tf_op jit(solution)/shard_map/pallas_call | solution.py:575
  26.8 0.8 %fusion = bf16[6,8,32,128]{3,2,1,0:T(8,128)(2,1)} fusion(f32[6,8,32,128]{3,2,1,0:T(8,128)S(1)} %shard_map.109), kind=kLoop, calls=%fused_computation.1 | loop fusion | flops 589824 | bytes 1179648 | tf_op jit(solution)/shard_map/convert_element_type | solution.py:24

commit v5 on v4

--- a/solution.py
+++ b/solution.py
@@ -329,8 +329,8 @@
         for a in range(3):
             rows = jnp.concatenate(
                 [
-                    taps[pl.ds(z + a, 2), pl.ds(r // 2, half_height), r % 2].reshape(
-                        2 * half_height * width, 3 * skip
+                    taps[z + a, pl.ds(r // 2, half_height), r % 2].reshape(
+                        half_height * width, 3 * skip
                     )
                     for r in range(4)
                 ],
@@ -387,20 +387,16 @@
         copy.wait()
     encode_bias = jnp.concatenate([b_encode[...], b_encode[...]], axis=-1)
 
-    def encode(i, carry):
-        z = 2 * i
+    def encode(z, carry):
         values = rounded(leaky_relu(pair_conv(v_taps, encode_pairs, z) + encode_bias))
-        values = values.reshape(2, half_height, width, 2 * skip)
-        for dz in range(2):
-            for y in range(height):
-                cells = values[dz, y // 2, :, (y % 2) * skip : (y % 2 + 1) * skip]
-                e_cells[z + dz + 1, y + 1] = cells
-                e_frame[(z + dz + 1) * slab + y + 1, lead : lead + width, :] = cells.astype(
-                    jnp.float32
-                )
+        values = values.reshape(half_height, width, 2 * skip)
+        for y in range(height):
+            cells = values[y // 2, :, (y % 2) * skip : (y % 2 + 1) * skip]
+            e_cells[z + 1, y + 1] = cells
+            e_frame[(z + 1) * slab + y + 1, lead : lead + width, :] = cells.astype(jnp.float32)
         return carry
 
-    lax.fori_loop(0, half_depth, encode, 0)
+    lax.fori_loop(0, depth, encode, 0)
 
     def gather_down(z, carry):
         for y in range(half_height):
@@ -448,7 +444,7 @@
     spread_own(e_frame, e_taps)
 
     def decode_skip(i, carry):
-        partial[i] = pair_conv(e_taps, skip_pairs, 2 * i)
+        partial[i] = pair_conv(e_taps, skip_pairs, i)
         return carry
 
     arrive(c_copies)
@@ -520,7 +516,7 @@
     spread_rest(e_frame, e_taps)
     for copy in skip_loads:
         copy.wait()
-    lax.fori_loop(0, half_depth, decode_skip, 0)
+    lax.fori_loop(0, depth, decode_skip, 0)
     arrive(r_copies)
     halo_to_frame(r_cells, r_frame, depth, height, width)
     arrive(r_edges)
@@ -531,14 +527,13 @@
     decode_bias = jnp.concatenate([b_decode[...], b_decode[...]], axis=-1)
 
     def decode(i, carry):
-        values = pair_conv(r_taps, raised_pairs, 2 * i) + partial[i]
-        values = (values + decode_bias).reshape(2, half_height, width, 2 * skip)
-        for dz in range(2):
-            for y in range(height):
-                decoded[2 * i + dz, y] = values[dz, y // 2, :, (y % 2) * skip : (y % 2 + 1) * skip]
+        values = pair_conv(r_taps, raised_pairs, i) + partial[i]
+        values = (values + decode_bias).reshape(half_height, width, 2 * skip)
+        for y in range(height):
+            decoded[i, y] = values[y // 2, :, (y % 2) * skip : (y % 2 + 1) * skip]
         return carry
 
-    lax.fori_loop(0, half_depth, decode, 0)
+    lax.fori_loop(0, depth, decode, 0)
     for going, copy in started:
         pl.when(going)(copy.wait_send)
 
@@ -607,7 +602,7 @@
             pltpu.VMEM(w_bottom.shape, half),
             pltpu.VMEM((deep, 8 * skip), half),
             pltpu.VMEM((half_depth, half_height, half_width, 8 * skip), half),
-            pltpu.VMEM((half_depth, height * width, 2 * skip), jnp.float32),
+            pltpu.VMEM((depth, height * width // 2, 2 * skip), jnp.float32),
             bias(skip),
             bias(deep),
             bias(deep),

time: 27.8 us -> 28.9 us (1.040)
  Pallas kernels: 26.8 us -> 27.9 us
    pallas_call x1, Pallas kernels: 26.8 us -> 27.9 us  [body(): pl.pallas_call(functools.partial(kernel, sizes), out_shape=jax.ShapeDtype...]
where the time goes in v5:
time: 28.9 us; the launch traced here: 28.7 us
  Pallas kernels  27.9 us (97%)
  other arithmetic  0.84 us (3%)
    pallas_call x1, Pallas kernels, body(): pl.pallas_call(functools.partial(kernel, sizes), out_shape=jax.ShapeDtype...  27.9 us
    convert_element_type x1, other arithmetic, rounded(): return values.astype(jnp.bfloat16)  0.84 us

profile of v5, /device:TPU:0, one launch (start us, length us, event | category | flops | bytes accessed | tf_op | source)
XLA Modules:
  0.0 28.7 jit_solution(12766719393126869869)
XLA Ops:
  0.0 27.9 %shard_map.109 = f32[6,8,32,128]{3,2,1,0:T(8,128)S(1)} custom-call(bf16[6,8,32,128]{3,2,1,0:T(8,128)(2,1)} %volume.1, bf16[3,3,3,128,128]{4,3,2,1,0:T(8,128)(2,1)} %w_encode.1, bf16[2,2,2,128,256]{4,3,2,1,0:T(8,128)(2,1)} %w_down.1, bf16[3,3,3,256,256]{4,3,2,1,0:T(8,128)(2,1)} %w_bottom.1, bf16[2,2,2,256,128]{4,3,2,1,0:T(8,128)(2,1)} %w_up.1, ...), custom_call_target="tpu_custom_call" | custom-call | tf_op jit(solution)/shard_map/pallas_call | solution.py:570
  27.9 0.8 %fusion = bf16[6,8,32,128]{3,2,1,0:T(8,128)(2,1)} fusion(f32[6,8,32,128]{3,2,1,0:T(8,128)S(1)} %shard_map.109), kind=kLoop, calls=%fused_computation.1 | loop fusion | flops 589824 | bytes 1179648 | tf_op jit(solution)/shard_map/convert_element_type | solution.py:24
